TPU v7x, 256 devices: a whole 4x4x8 slice. The times are simulated.
256 devices in a mesh: rep: 8 (over z), exp: 32 (over y, x, core).
Axes of the slice: x: 4, y: 4, z: 8, core: 2. Of those that a mesh axis runs over, the one named last changes fastest.
Arguments:
- tokens: bfloat16 [16384, 7168], P(('rep', 'exp')), may hold values from -6 to 6
- expert_ids: int32 [16384, 2], P(('rep', 'exp')), may hold values from 0 to 31, as said below
- combine_weights: bfloat16 [16384, 2], P(('rep', 'exp')), may hold values from 0.19921875 to 1
- gate_up_weight: bfloat16 [32, 7168, 2, 1024], P('exp', 'rep'), may hold values from -0.0625 to 0.0625
- down_weight: bfloat16 [32, 1024, 7168], P('exp', None, 'rep'), may hold values from -0.1875 to 0.1875
Outputs:
- combined: float32 [16384, 7168], P(('rep', 'exp'))
- hessian: float32 [32, 1024, 1024], P('exp', 'rep')
Inputs may be any that keep to these rules, and one draw needn't show every extreme that they name: `expert_ids`: the 2 experts of a token differ. Among the 64 rows of one device no expert is named by more than 4 rows, and on every device some expert is named exactly 4 times.
All inputs are finite; a program needn't handle non-finite values.
Results may differ from a plain program's by a relative error of at most 0.0041.
Values may be sent and summed in bfloat16 or wider, within the bound.
A program may use at most 64 MiB of HBM per device.

v0:
```python
import jax
import jax.numpy as jnp
from jax import lax
from jax.sharding import PartitionSpec as P


def local(tokens, expert_ids, combine_weights, gate_up_weight, down_weight):
    tok_rows, width = tokens.shape
    routes_each = expert_ids.shape[1]
    experts = lax.axis_size("exp")
    replicas = lax.axis_size("rep")
    capacity = max(2, 9 * tok_rows * routes_each // (8 * experts))
    slots_all = experts * capacity
    rows_all = replicas * slots_all
    hidden_units = down_weight.shape[1]
    flat_ids = expert_ids.reshape(-1)
    onehot = (flat_ids[:, None] == jnp.arange(experts, dtype=jnp.int32)[None, :]).astype(jnp.int32)
    rank = jnp.sum((jnp.cumsum(onehot, axis=0) - onehot) * onehot, axis=1)
    position = flat_ids * capacity + rank
    placed = (position[:, None] == jnp.arange(slots_all, dtype=jnp.int32)[None, :]).reshape(
        tok_rows, routes_each, slots_all
    )
    dispatch_matrix = jnp.any(placed, axis=1).astype(jnp.bfloat16)
    combine_matrix = jnp.sum(
        placed.astype(jnp.float32) * combine_weights.astype(jnp.float32)[:, :, None], axis=1
    ).astype(jnp.bfloat16)
    outgoing = lax.dot_general(
        dispatch_matrix, tokens, (((0,), (0,)), ((), ())), preferred_element_type=jnp.float32
    )
    outgoing = outgoing.astype(jnp.bfloat16).reshape(1, experts, capacity, width)
    arrived = lax.all_to_all(
        lax.all_to_all(outgoing, "exp", split_axis=1, concat_axis=1, tiled=True),
        "rep",
        split_axis=3,
        concat_axis=0,
        tiled=True,
    )
    token_rows = arrived.reshape(rows_all, arrived.shape[3])
    joined = gate_up_weight.reshape(gate_up_weight.shape[1], 2 * hidden_units)
    preact = lax.psum_scatter(
        jnp.dot(token_rows, joined, preferred_element_type=jnp.float32),
        "rep",
        scatter_dimension=0,
        tiled=True,
    )
    hidden = (jax.nn.silu(preact[:, :hidden_units]) * preact[:, hidden_units:]).astype(jnp.bfloat16)
    down_local = down_weight[0]
    scale = 2.0 / rows_all
    partial_hess = lax.dot_general(
        hidden, hidden, (((0,), (0,)), ((), ())), preferred_element_type=jnp.float32
    )
    hess_block = lax.psum_scatter(partial_hess, "rep", scatter_dimension=0, tiled=True)
    expert_rows = jnp.dot(
        lax.all_gather(hidden, "rep", axis=0, tiled=True),
        down_local,
        preferred_element_type=jnp.float32,
    ).astype(jnp.bfloat16)
    hessian = (hess_block * scale)[None]
    produced_all = expert_rows.reshape(replicas, experts, capacity, expert_rows.shape[1])
    coming = lax.all_to_all(
        lax.all_to_all(produced_all, "rep", split_axis=0, concat_axis=3, tiled=True),
        "exp",
        split_axis=1,
        concat_axis=1,
        tiled=True,
    )
    back_rows = coming.reshape(slots_all, width)
    combined = jnp.dot(combine_matrix, back_rows, preferred_element_type=jnp.float32)
    return (combined, hessian)


def solution(mesh):
    return jax.shard_map(
        local,
        mesh=mesh,
        in_specs=(
            P(("rep", "exp"), None),
            P(("rep", "exp"), None),
            P(("rep", "exp"), None),
            P("exp", "rep", None, None),
            P("exp", None, "rep"),
        ),
        out_specs=(P(("rep", "exp"), None), P("exp", "rep", None)),
        check_vma=False,
    )
```

profile of v0, /device:TPU:1, one launch (start us, length us, event | category | flops | bytes accessed | tf_op | source)
XLA Modules:
  0.0 425.1 jit_solution(9704095627140846401)
XLA Ops:
  7.2 0.9 copy.46
  8.9 0.7 multiply_add_fusion
  9.7 3.1 convolution_convert_fusion
  12.8 4.1 reshape.40
  16.8 34.1 %all_to_all.43 = bf16[1,32,4,7168]{3,2,0,1:T(4,128)(2,1)} all-to-all(bf16[1,32,4,7168]{3,2,0,1:T(4,128)(2,1)} %bitcast.35), channel_id=1, replica_groups=mesh['rep'=8,'exp'=32] {'exp'}, dimensions={1} | all-to-all | bytes 3670016 | tf_op jit(solution)/shard_map/all_to_all | solution.py:32
  51.0 11.8 %copy.49 = bf16[1,32,4,7168]{1,2,0,3:T(4,128)(2,1)} copy(bf16[1,32,4,7168]{3,2,0,1:T(4,128)(2,1)} %all_to_all.43) | data formatting | bytes 3670016 | tf_op jit(solution)/shard_map/all_to_all | solution.py:32
  62.8 10.4 %reshape.46 = bf16[8,2,57344]{2,1,0:T(2,128)(2,1)} reshape(bf16[7168,1,4,32]{3,2,1,0:T(4,128)(2,1)} %bitcast.33) | data formatting | bytes 3670016
  73.2 8.2 %all-to-all-start.1 = ((bf16[8,2,57344]{2,1,0:T(2,128)(2,1)}), bf16[8,2,57344]{2,1,0:T(2,128)(2,1)}, u32[]{:S(2)}, u32[]{:S(2)}) async-start(bf16[8,2,57344]{2,1,0:T(2,128)(2,1)} %reshape.46), calls=%async_computation.1 | async-start | bytes 3670016 | tf_op jit(solution)/shard_map/all_to_all | solution.py:31
  81.4 5.1 %copy.58 = bf16[112,8,2,1024]{3,1,2,0:T(8,128)(2,1)} copy(bf16[112,8,2,1024]{3,2,1,0:T(2,128)(2,1)} %bitcast.38) | data formatting | bytes 7340032
  86.5 38.2 %all-to-all-done.1 = bf16[8,2,57344]{2,1,0:T(2,128)(2,1)} async-done(((bf16[8,2,57344]{2,1,0:T(2,128)(2,1)}), bf16[8,2,57344]{2,1,0:T(2,128)(2,1)}, u32[]{:S(2)}, u32[]{:S(2)}) %all-to-all-start.1) | async-done | bytes 1835040 | tf_op jit(solution)/shard_map/all_to_all | solution.py:31
  124.6 8.5 %reshape.47 = bf16[7168,1,4,32]{3,2,1,0:T(4,128)(2,1)} reshape(bf16[8,2,57344]{2,1,0:T(2,128)(2,1)} %all-to-all-done.1) | data formatting | bytes 3670016
  133.1 8.7 %copy.55 = bf16[1,32,4,8,896]{4,3,1,2,0:T(8,128)(2,1)} copy(bf16[1,32,4,8,896]{1,2,4,3,0:T(4,128)(2,1)} %bitcast.34) | data formatting | bytes 3670016 | tf_op jit(solution)/shard_map/all_to_all | solution.py:31
  141.7 4.2 copy.51
  145.9 4.0 reshape.41
  149.9 10.4 %fusion.10 = f32[1024,2048]{1,0:T(8,128)} fusion(bf16[1024,896]{1,0:T(8,128)(2,1)} %reshape.41, bf16[896,2048]{1,0:T(8,128)(2,1)} %bitcast.39), kind=kOutput, calls=%fused_computation.16 | convolution fusion | flops 3758096384 | bytes 13893632 | tf_op jit(solution)/shard_map/dot_general | solution.py:41
  160.4 90.8 %reduce-scatter.3.cloned.1.call-done = f32[128,2048]{1,0:T(8,128)} async-done(((f32[1024,2048]{1,0:T(8,128)}), f32[128,2048]{1,0:T(8,128)}) %reduce-scatter.3.cloned.1.call-update) | async-done | bytes 1048592 | tf_op jit(solution)/shard_map/reduce_scatter | solution.py:40
  251.1 2.1 fusion.5
  253.2 0.2 reduce-scatter.5.cloned.1.call-start
  253.5 3.7 fusion.11
  257.2 32.4 %all-gather.2.cloned.1.call-done = bf16[1024,1024]{1,0:T(8,128)(2,1)} async-done(((bf16[128,1024]{1,0:T(8,128)(2,1)}), bf16[1024,1024]{1,0:T(8,128)(2,1)}) %all-gather.2.cloned.1.call-update) | async-done | bytes 2097168 | tf_op jit(solution)/shard_map/all_gather | solution.py:54
  289.6 5.1 %fusion.2 = bf16[1024,896]{1,0:T(8,128)(2,1)} fusion(bf16[1024,1024]{1,0:T(8,128)(2,1)} %all-gather.2.cloned.1.call-done, bf16[1,1024,896]{2,1,0:T(8,128)(2,1)S(1)} %copy-done), kind=kOutput, calls=%fused_computation.3 | convolution fusion | flops 1879965696 | bytes 5767168 | tf_op jit(solution)/shard_map/dot_general | solution.py:53
  294.7 4.1 reshape.43
  298.8 1.8 copy.52
  300.6 66.9 %all_to_all.44 = bf16[8,32,4,896]{3,1,2,0:T(8,128)(2,1)S(1)} all-to-all(bf16[8,32,4,896]{3,1,2,0:T(8,128)(2,1)S(1)} %copy.52), channel_id=1, replica_groups=mesh['rep'=8,'exp'=32] {'rep'}, dimensions={0} | all-to-all | bytes 3670016 | tf_op jit(solution)/shard_map/all_to_all | solution.py:61
  367.5 2.3 copy.56
  369.8 4.3 %reshape.45 = bf16[1,32,4,7168]{3,2,0,1:T(4,128)(2,1)} reshape(bf16[1,32,4,8,896]{4,3,2,1,0:T(8,128)(2,1)} %copy.56) | data formatting | bytes 3670016 | tf_op jit(solution)/shard_map/all_to_all | solution.py:61
  374.1 12.4 %all-to-all-start.3 = ((bf16[1,32,4,7168]{3,2,0,1:T(4,128)(2,1)}), bf16[1,32,4,7168]{3,2,0,1:T(4,128)(2,1)}, u32[]{:S(2)}, u32[]{:S(2)}) async-start(bf16[1,32,4,7168]{3,2,0,1:T(4,128)(2,1)} %reshape.45), calls=%async_computation.4 | async-start | bytes 3670016 | tf_op jit(solution)/shard_map/all_to_all | solution.py:60
  386.6 1.7 reduce-scatter.5.cloned.1.call-done
  388.3 1.9 multiply_bitcast_fusion
  390.2 21.3 %all-to-all-done.3 = bf16[1,32,4,7168]{3,2,0,1:T(4,128)(2,1)} async-done(((bf16[1,32,4,7168]{3,2,0,1:T(4,128)(2,1)}), bf16[1,32,4,7168]{3,2,0,1:T(4,128)(2,1)}, u32[]{:S(2)}, u32[]{:S(2)}) %all-to-all-start.3) | async-done | bytes 1835040 | tf_op jit(solution)/shard_map/all_to_all | solution.py:60
  411.4 4.0 reshape.44
  415.4 3.1 fusion.12
  (18 shorter events, 1.1 us)
Async XLA Ops:
  7.2 282.4 %copy-start = (bf16[1,1024,896]{2,1,0:T(8,128)(2,1)S(1)}, bf16[1,1024,896]{2,1,0:T(8,128)(2,1)}, u32[]{:S(2)}) copy-start(bf16[1,1024,896]{2,1,0:T(8,128)(2,1)} %param.9) | copy-start | bytes 5505028
  73.2 51.5 %all-to-all-start.1 = ((bf16[8,2,57344]{2,1,0:T(2,128)(2,1)}), bf16[8,2,57344]{2,1,0:T(2,128)(2,1)}, u32[]{:S(2)}, u32[]{:S(2)}) async-start(bf16[8,2,57344]{2,1,0:T(2,128)(2,1)} %reshape.46), calls=%async_computation.1 | async-start | bytes 3670016 | tf_op jit(solution)/shard_map/all_to_all | solution.py:31
  81.3 169.8 %reduce-scatter.3.cloned.1.call-start = ((), (), s32[]{:S(2)}) async-start(), calls=%async_computation.6 | async-start | bytes 9437184 | tf_op jit(solution)/shard_map/reduce_scatter | solution.py:40
  160.3 129.2 %all-gather.2.cloned.1.call-start = ((), (), s32[]{:S(2)}) async-start(), calls=%async_computation.7 | async-start | bytes 2359296 | tf_op jit(solution)/shard_map/all_gather | solution.py:54
  253.2 135.1 %reduce-scatter.5.cloned.1.call-start = ((), (), s32[]{:S(2)}) async-start(), calls=%async_computation.8 | async-start | bytes 4718592 | tf_op jit(solution)/shard_map/reduce_scatter | solution.py:52
  374.1 12.4 %copy-start.1 = (bf16[64,2]{0,1:T(2,128)(2,1)S(1)}, bf16[64,2]{0,1:T(2,128)(2,1)}, u32[]{:S(2)}) copy-start(bf16[64,2]{0,1:T(2,128)(2,1)} %param.7) | copy-start | bytes 772
  374.1 37.4 %all-to-all-start.3 = ((bf16[1,32,4,7168]{3,2,0,1:T(4,128)(2,1)}), bf16[1,32,4,7168]{3,2,0,1:T(4,128)(2,1)}, u32[]{:S(2)}, u32[]{:S(2)}) async-start(bf16[1,32,4,7168]{3,2,0,1:T(4,128)(2,1)} %reshape.45), calls=%async_computation.4 | async-start | bytes 3670016 | tf_op jit(solution)/shard_map/all_to_all | solution.py:60
Sparse Core Ops, SparseCore 0:
  160.4 90.6 reduce-scatter.2
  253.5 36.0 all-gather.1
  292.1 96.1 reduce-scatter.4
where the time goes:
time: 427 us; the launch traced here: 425 us
  waiting for transfers between devices  184 us (43%)
  blocking collectives  101 us (24%)
  local copies, waits for them, and re-layouts  74.3 us (17%)
  matrix products  25.5 us (6%)
  starting transfers between devices  20.9 us (5%)
  between operations  13.8 us (3%)
  other arithmetic  5.25 us (1%)
    reduce_scatter x1, waiting for transfers between devices, local(): lax.psum_scatter(jnp.dot(token_rows, joined, preferred_element_type=jnp.f...  90.8 us
    all_to_all x1, blocking collectives, local(): lax.all_to_all(produced_all, 'rep', split_axis=0, concat_axis=3, tiled=True)  66.9 us
    all_to_all x1, waiting for transfers between devices, local(): lax.all_to_all(lax.all_to_all(outgoing, 'exp', split_axis=1, concat_axis=...  38.2 us
    all_to_all x1, blocking collectives, local(): lax.all_to_all(outgoing, 'exp', split_axis=1, concat_axis=1, tiled=True)  34.1 us
    all_gather x1, waiting for transfers between devices, local(): lax.all_gather(hidden, 'rep', axis=0, tiled=True)  32.4 us
    unnamed x8, local copies, waits for them, and re-layouts  24.8 us
    all_to_all x1, waiting for transfers between devices, local(): lax.all_to_all(lax.all_to_all(produced_all, 'rep', split_axis=0, concat_a...  21.3 us
    all_to_all x2, local copies, waits for them, and re-layouts, local(): lax.all_to_all(lax.all_to_all(outgoing, 'exp', split_axis=1, concat_axis=...  12.8 us
  transfers between devices with their start and end apart: 5, of which 5 were waited for; matrix products, arithmetic and copies ran while one was open for 7% of the time, Pallas kernels for 0%

commit v1 on v0

v1 whole, which is shorter than its diff:
```python
import functools

import jax
import jax.numpy as jnp
from jax import lax
from jax.experimental import pallas as pl
from jax.experimental.pallas import tpu as pltpu
from jax.sharding import PartitionSpec as P

MESH = pl.DeviceIdType.MESH
Z = 8
E = 32
TOK = 64
SLOT = 4
D = 7168
DS = D // Z
FF = 1024
ROWS = 512
BLK = 16
CH = ROWS // Z
NSUB = 2
SUB = CH // NSUB
MSG = 2 * FF + 128
LEVELS = 32000.0
FAR = ((4, 3), (3, 4))


def kernel(
    tok, meta, w3, dn, comb_out, hess_out,
    T, M, DM, CT, G, X, W3V, W, DN, PRE, RSS, RSR, HD, OUT, B, CB,
    loc, p1s, p1r, m1s, m1r, p3s, p3r, rss, rsr, ags, agr, p8s, p8r, p10s, p10r,
):
    r = lax.axis_index("rep")
    i = lax.axis_index("exp")
    odd = lax.rem(r, 2)
    cl_own = r // 2

    def zdev(k):
        return lax.rem(r + k + Z, Z)

    w_copy = pltpu.make_async_copy(w3, W3V, loc.at[0])
    dn_copy = pltpu.make_async_copy(dn, DN, loc.at[1])
    own_copy = pltpu.make_async_copy(
        tok.at[:, pl.ds(pl.multiple_of(r * DS, 128), DS)],
        T.at[odd, pl.ds(pl.multiple_of(cl_own * TOK, TOK), TOK)],
        loc.at[2],
    )
    own_meta = pltpu.make_async_copy(meta, M.at[odd, cl_own], loc.at[3])
    own_copy.start()
    own_meta.start()
    w_copy.start()
    dn_copy.start()

    barrier = pltpu.get_barrier_semaphore()

    @pl.loop(1, Z)
    def _(k):
        pl.semaphore_signal(barrier, inc=1, device_id=(zdev(k), i), device_id_type=MESH)

    @pl.loop(1, E)
    def _(k):
        pl.semaphore_signal(barrier, inc=1, device_id=(r, lax.rem(i + k, E)), device_id_type=MESH)

    pl.semaphore_wait(barrier, Z - 1 + E - 1)

    def p1_pair(k):
        to = zdev(k)
        a = pltpu.make_async_remote_copy(
            src_ref=tok.at[:, pl.ds(pl.multiple_of(to * DS, 128), DS)],
            dst_ref=T.at[odd, pl.ds(pl.multiple_of(cl_own * TOK, TOK), TOK)],
            send_sem=p1s.at[k],
            recv_sem=p1r.at[odd, cl_own],
            device_id=(to, i),
            device_id_type=MESH,
        )
        b = pltpu.make_async_remote_copy(
            src_ref=meta,
            dst_ref=M.at[odd, cl_own],
            send_sem=m1s.at[k],
            recv_sem=m1r.at[odd, cl_own],
            device_id=(to, i),
            device_id_type=MESH,
        )
        return a, b

    def p1_send():
        @pl.loop(1, Z)
        def _(k):
            a, b = p1_pair(k)
            b.start()
            a.start()

    def p1_wait(h):
        for cl in range(4):
            @pl.when(r != 2 * cl + h)
            def _():
                pltpu.make_async_remote_copy(
                    src_ref=T.at[h, pl.ds(cl * TOK, TOK)],
                    dst_ref=T.at[h, pl.ds(cl * TOK, TOK)],
                    send_sem=p1s.at[0],
                    recv_sem=p1r.at[h, cl],
                    device_id=(zdev(1), i),
                    device_id_type=MESH,
                ).wait_recv()
                pltpu.make_async_remote_copy(
                    src_ref=meta,
                    dst_ref=M.at[h, cl],
                    send_sem=m1s.at[0],
                    recv_sem=m1r.at[h, cl],
                    device_id=(zdev(1), i),
                    device_id_type=MESH,
                ).wait_recv()

    def gather(h):
        rows = lax.broadcasted_iota(jnp.int32, (ROWS, 128), 0).astype(jnp.float32)
        for p in range(2):
            m = jnp.maximum(M[h, 2 * p], M[h, 2 * p + 1])
            hit0 = rows == m[0:1, :]
            hit1 = rows == m[1:2, :]
            DM[:, p * 128:(p + 1) * 128] = jnp.where(hit0 | hit1, 1.0, 0.0).astype(jnp.bfloat16)
            CT[h, :, p * 128:(p + 1) * 128] = (
                jnp.where(hit0, m[2:3, :], 0.0) + jnp.where(hit1, m[3:4, :], 0.0)
            ).astype(jnp.bfloat16)

        @pl.loop(0, 4)
        def _(q):
            at = pl.ds(pl.multiple_of(q * 128, 128), 128)
            G[h, at, :] = jnp.dot(DM[at, :], T[h], preferred_element_type=jnp.float32).astype(jnp.bfloat16)

    def plane_copy(src, dst, h, k, ssem, rsem):
        to = lax.rem(i + k, E)
        return pltpu.make_async_remote_copy(
            src_ref=src.at[h, pl.ds(pl.multiple_of(to * BLK, BLK), BLK)],
            dst_ref=dst.at[h, pl.ds(pl.multiple_of(i * BLK, BLK), BLK)],
            send_sem=ssem.at[h],
            recv_sem=rsem.at[h],
            device_id=(r, to),
            device_id_type=MESH,
        )

    def plane_send(src, dst, h, ssem, rsem):
        @pl.loop(1, E)
        def _(k):
            plane_copy(src, dst, h, k, ssem, rsem).start()

        own = pl.ds(pl.multiple_of(i * BLK, BLK), BLK)
        dst[h, own, :] = src[h, own, :]

    def plane_all(src, dst, h, ssem, rsem):
        most = pl.ds(0, ROWS - BLK)
        return pltpu.make_async_remote_copy(
            src_ref=src.at[h, most],
            dst_ref=dst.at[h, most],
            send_sem=ssem.at[h],
            recv_sem=rsem.at[h],
            device_id=(r, lax.rem(i + 1, E)),
            device_id_type=MESH,
        )

    def up(h):
        @pl.loop(0, 8)
        def _(n):
            at = pl.ds(pl.multiple_of(n * 256, 256), 256)
            PRE[h, :, at] = jnp.dot(X[h], W[:, at], preferred_element_type=jnp.float32)

    def rs_copy(h, way, sub, d):
        step = 1 if way == 0 else -1
        return pltpu.make_async_remote_copy(
            src_ref=RSS.at[h, way, sub, d - 1],
            dst_ref=RSR.at[h, way, sub, d - 1],
            send_sem=rss.at[h, way, sub, d - 1],
            recv_sem=rsr.at[h, way, sub, d - 1],
            device_id=(zdev(step), i),
            device_id_type=MESH,
        )

    def decode(h, way, sub, d):
        q = RSR[h, way, sub, d - 1]
        scale = jnp.exp2(q[:, 2 * FF:].astype(jnp.float32)) * (1.0 / LEVELS)
        return q, scale

    def rs_send(h, way, sub, d):
        owner = zdev(d if way == 0 else -d)
        at = pl.ds(pl.multiple_of(owner * CH + sub * SUB, SUB), SUB)
        far = FAR[h][way]
        s = PRE[h, at, :]
        if d < far:
            rs_copy(h, way, sub, d + 1).wait_recv()
            q, scale = decode(h, way, sub, d + 1)
            s = s + q[:, :2 * FF].astype(jnp.float32) * jnp.tile(scale, (1, 16))
        most = jnp.maximum(jnp.max(jnp.abs(s), axis=1, keepdims=True), 1e-30)
        expo = jnp.ceil(jnp.log2(most))
        code = jnp.round(s * (jnp.exp2(-expo) * LEVELS))
        RSS[h, way, sub, d - 1, :, :2 * FF] = code.astype(jnp.int32).astype(jnp.int16)
        RSS[h, way, sub, d - 1, :, 2 * FF:] = jnp.broadcast_to(expo, (SUB, 128)).astype(jnp.int32).astype(jnp.int16)
        rs_copy(h, way, sub, d).start()

    def ag_copy(h, way, sub, k):
        step = 1 if way == 0 else -1
        origin = zdev(-(k - 1) * step)
        at = pl.ds(pl.multiple_of(origin * CH + sub * SUB, SUB), SUB)
        return pltpu.make_async_remote_copy(
            src_ref=HD.at[h, at],
            dst_ref=HD.at[h, at],
            send_sem=ags.at[h, way, sub, k - 1],
            recv_sem=agr.at[h, way, sub, k - 1],
            device_id=(zdev(step), i),
            device_id_type=MESH,
        )

    def ag_wait(h, way, sub, k):
        step = 1 if way == 0 else -1
        origin = zdev(-k * step)
        at = pl.ds(pl.multiple_of(origin * CH + sub * SUB, SUB), SUB)
        pltpu.make_async_remote_copy(
            src_ref=HD.at[h, at],
            dst_ref=HD.at[h, at],
            send_sem=ags.at[h, way, sub, k - 1],
            recv_sem=agr.at[h, way, sub, k - 1],
            device_id=(zdev(step), i),
            device_id_type=MESH,
        ).wait_recv()

    def finish(h, sub):
        at = pl.ds(pl.multiple_of(r * CH + sub * SUB, SUB), SUB)
        s = PRE[h, at, :]
        for way in range(2):
            rs_copy(h, way, sub, 1).wait_recv()
            q, scale = decode(h, way, sub, 1)
            s = s + q[:, :2 * FF].astype(jnp.float32) * jnp.tile(scale, (1, 16))
        g = s[:, :FF]
        HD[h, at, :] = (g / (1.0 + jnp.exp(-g)) * s[:, FF:]).astype(jnp.bfloat16)
        for way in range(2):
            ag_copy(h, way, sub, 1).start()

    def ag_step(h, way, sub, k):
        ag_wait(h, way, sub, k)
        if k < FAR[h][way]:
            ag_copy(h, way, sub, k + 1).start()

    def down(h):
        @pl.loop(0, 7)
        def _(n):
            at = pl.ds(pl.multiple_of(n * 128, 128), 128)
            OUT[h, :, at] = jnp.dot(HD[h], DN[:, at], preferred_element_type=jnp.float32).astype(jnp.bfloat16)

    def combine(h):
        CB[h] = lax.dot_general(
            CT[h], B[h], (((0,), (0,)), ((), ())), preferred_element_type=jnp.float32
        ).astype(jnp.bfloat16)

    mine = pl.ds(pl.multiple_of(r * DS, 128), DS)

    def p10_copy(h, cl):
        return pltpu.make_async_remote_copy(
            src_ref=CB.at[h, pl.ds(cl * TOK, TOK)],
            dst_ref=comb_out.at[:, mine],
            send_sem=p10s.at[h, cl],
            recv_sem=p10r.at[r],
            device_id=(2 * cl + h, i),
            device_id_type=MESH,
        )

    def p10_self(h, cl):
        return pltpu.make_async_copy(CB.at[h, pl.ds(cl * TOK, TOK)], comb_out.at[:, mine], loc.at[4])

    def p10_send(h):
        for cl in range(4):
            @pl.when(r != 2 * cl + h)
            def _():
                p10_copy(h, cl).start()

            @pl.when(r == 2 * cl + h)
            def _():
                p10_self(h, cl).start()

    def hessian():
        at = pl.ds(pl.multiple_of(r * 128, 128), 128)
        total = lax.dot_general(
            HD[0, :, at], HD[0], (((0,), (0,)), ((), ())), preferred_element_type=jnp.float32
        ) + lax.dot_general(
            HD[1, :, at], HD[1], (((0,), (0,)), ((), ())), preferred_element_type=jnp.float32
        )
        hess_out[...] = total * (2.0 / 1024.0)

    @pl.when(odd == 0)
    def _():
        p1_send()

    w_copy.wait()

    @pl.loop(0, 14)
    def _(n):
        at = pl.ds(pl.multiple_of(n * 64, 64), 64)
        W[at, :FF] = W3V[at, 0, :]
        W[at, FF:] = W3V[at, 1, :]

    own_copy.wait()
    own_meta.wait()
    p1_wait(0)

    @pl.when(odd == 1)
    def _():
        p1_send()

    gather(0)
    plane_send(G, X, 0, p3s, p3r)
    p1_wait(1)
    gather(1)
    plane_send(G, X, 1, p3s, p3r)

    def rs_round(h, steps):
        for back in steps:
            for sub in range(NSUB):
                for way in range(2):
                    d = FAR[h][way] - back
                    if d >= 1:
                        rs_send(h, way, sub, d)

    plane_all(G, X, 0, p3s, p3r).wait_recv()
    up(0)
    rs_round(0, [0, 1])
    plane_all(G, X, 1, p3s, p3r).wait_recv()
    up(1)
    rs_round(0, [2])
    rs_round(1, [0])
    rs_round(0, [3])
    for sub in range(NSUB):
        finish(0, sub)
    rs_round(1, [1])
    for k in range(1, 5):
        for sub in range(NSUB):
            for way in range(2):
                if k <= FAR[0][way]:
                    ag_step(0, way, sub, k)
        if k == 1:
            rs_round(1, [2])
        if k == 3:
            rs_round(1, [3])
            for sub in range(NSUB):
                finish(1, sub)
    dn_copy.wait()
    down(0)
    plane_send(OUT, B, 0, p8s, p8r)
    for k in range(1, 5):
        for sub in range(NSUB):
            for way in range(2):
                if k <= FAR[1][way]:
                    ag_step(1, way, sub, k)
    down(1)
    plane_send(OUT, B, 1, p8s, p8r)
    hessian()
    for h in range(2):
        plane_all(OUT, B, h, p8s, p8r).wait_recv()
        combine(h)
        p10_send(h)

    @pl.loop(1, Z)
    def _(k):
        a, b = p1_pair(k)
        a.wait_send()
        b.wait_send()

    for h in range(2):
        plane_all(G, X, h, p3s, p3r).wait_send()
        plane_all(OUT, B, h, p8s, p8r).wait_send()
        for way in range(2):
            for sub in range(NSUB):
                for d in range(1, FAR[h][way] + 1):
                    rs_copy(h, way, sub, d).wait_send()
                    ag_copy(h, way, sub, d).wait_send()
        for cl in range(4):
            @pl.when(r != 2 * cl + h)
            def _():
                p10_copy(h, cl).wait_send()

            @pl.when(r == 2 * cl + h)
            def _():
                p10_self(h, cl).wait()

    @pl.loop(1, Z)
    def _(k):
        src = zdev(k)
        pltpu.make_async_remote_copy(
            src_ref=CB.at[0, pl.ds(0, TOK)],
            dst_ref=comb_out.at[:, pl.ds(pl.multiple_of(src * DS, 128), DS)],
            send_sem=p10s.at[0, 0],
            recv_sem=p10r.at[src],
            device_id=(zdev(1), i),
            device_id_type=MESH,
        ).wait_recv()


def local(tokens, expert_ids, combine_weights, gate_up_weight, down_weight):
    r = lax.axis_index("rep")
    flat = expert_ids.reshape(-1)
    onehot = (flat[:, None] == jnp.arange(E, dtype=jnp.int32)[None, :]).astype(jnp.int32)
    rank = jnp.sum((jnp.cumsum(onehot, axis=0) - onehot) * onehot, axis=1)
    pos = (flat * BLK + (r // 2) * SLOT + rank).reshape(TOK, 2).astype(jnp.float32).T
    wts = combine_weights.astype(jnp.float32).T
    both = jnp.concatenate([pos, wts, jnp.zeros((4, TOK), jnp.float32)], axis=0)
    fill = jnp.concatenate(
        [jnp.full((2, TOK), -1.0, jnp.float32), jnp.zeros((6, TOK), jnp.float32)], axis=0
    )
    meta = jnp.where(
        lax.rem(r // 2, 2) == 0,
        jnp.concatenate([both, fill], axis=1),
        jnp.concatenate([fill, both], axis=1),
    )
    bf, f32 = jnp.bfloat16, jnp.float32
    dma = pltpu.SemaphoreType.DMA
    comb, hess = pl.pallas_call(
        kernel,
        out_shape=(
            jax.ShapeDtypeStruct((TOK, D), bf),
            jax.ShapeDtypeStruct((128, FF), f32),
        ),
        in_specs=[
            pl.BlockSpec(memory_space=pl.ANY),
            pl.BlockSpec(memory_space=pltpu.VMEM),
            pl.BlockSpec(memory_space=pl.ANY),
            pl.BlockSpec(memory_space=pl.ANY),
        ],
        out_specs=(
            pl.BlockSpec(memory_space=pl.ANY),
            pl.BlockSpec(memory_space=pltpu.VMEM),
        ),
        scratch_shapes=[
            pltpu.VMEM((2, 4 * TOK, DS), bf),
            pltpu.VMEM((2, 4, 8, 128), f32),
            pltpu.VMEM((ROWS, 4 * TOK), bf),
            pltpu.VMEM((2, ROWS, 4 * TOK), bf),
            pltpu.VMEM((2, ROWS, DS), bf),
            pltpu.VMEM((2, ROWS, DS), bf),
            pltpu.VMEM((DS, 2, FF), bf),
            pltpu.VMEM((DS, 2 * FF), bf),
            pltpu.VMEM((FF, DS), bf),
            pltpu.VMEM((2, ROWS, 2 * FF), f32),
            pltpu.VMEM((2, 2, NSUB, 4, SUB, MSG), jnp.int16),
            pltpu.VMEM((2, 2, NSUB, 4, SUB, MSG), jnp.int16),
            pltpu.VMEM((2, ROWS, FF), bf),
            pltpu.VMEM((2, ROWS, DS), bf),
            pltpu.VMEM((2, ROWS, DS), bf),
            pltpu.VMEM((2, 4 * TOK, DS), bf),
            dma((5,)),
            dma((Z,)),
            dma((2, 4)),
            dma((Z,)),
            dma((2, 4)),
            dma((2,)),
            dma((2,)),
            dma((2, 2, NSUB, 4)),
            dma((2, 2, NSUB, 4)),
            dma((2, 2, NSUB, 4)),
            dma((2, 2, NSUB, 4)),
            dma((2,)),
            dma((2,)),
            dma((2, 4)),
            dma((Z,)),
        ],
        compiler_params=pltpu.CompilerParams(
            collective_id=0, has_side_effects=True, vmem_limit_bytes=60 * 1024 * 1024
        ),
        name="moe",
    )(tokens, meta, gate_up_weight[0], down_weight[0])
    return comb.astype(jnp.float32), hess[None]


def solution(mesh):
    return jax.shard_map(
        local,
        mesh=mesh,
        in_specs=(
            P(("rep", "exp"), None),
            P(("rep", "exp"), None),
            P(("rep", "exp"), None),
            P("exp", "rep", None, None),
            P("exp", None, "rep"),
        ),
        out_specs=(P(("rep", "exp"), None), P("exp", "rep", None)),
        check_vma=False,
    )
```

time: 427 us -> 163 us (0.38)
  waiting for transfers between devices: 184 us -> 0 us
  Pallas kernels: 0 us -> 153 us
  blocking collectives: 101 us -> 0 us
  local copies, waits for them, and re-layouts: 74.3 us -> 1.91 us
  matrix products: 25.5 us -> 0 us
  starting transfers between devices: 20.9 us -> 0 us
  between operations: 13.8 us -> 0.7 us
    pallas_call x0 -> x1, Pallas kernels: none -> 153 us  [local(): pl.pallas_call(kernel, out_shape=(jax.ShapeDtypeStruct((TOK, D), bf), jax...]
    all_to_all x2 -> x0, blocking collectives: 101 us -> none  [the longest x1 66.9 us: local(): lax.all_to_all(produced_all, 'rep', split_axis=0, concat_axis=3, tiled=True)]
    reduce_scatter x2 -> x0, waiting for transfers between devices: 92.5 us -> none  [the longest x1 90.8 us: local(): lax.psum_scatter(jnp.dot(token_rows, joined, preferred_element_type=jnp.f...]
    all_to_all x2 -> x0, waiting for transfers between devices: 59.4 us -> none  [the longest x1 38.2 us: local(): lax.all_to_all(lax.all_to_all(outgoing, 'exp', split_axis=1, concat_axis=...]
    all_gather x1 -> x0, waiting for transfers between devices: 32.4 us -> none  [local(): lax.all_gather(hidden, 'rep', axis=0, tiled=True)]
    all_to_all x5 -> x0, local copies, waits for them, and re-layouts: 31.2 us -> none  [the longest x2 12.8 us: local(): lax.all_to_all(lax.all_to_all(outgoing, 'exp', split_axis=1, concat_axis=...]
    dot_general x5 -> x0, matrix products: 25.5 us -> none  [the longest x1 10.4 us: local(): jnp.dot(token_rows, joined, preferred_element_type=jnp.float32)]
    unnamed x8 -> x4, local copies, waits for them, and re-layouts: 24.8 us -> 1.56 us
  transfers between devices with their start and end apart: 5 -> 0, of which waited for: 5 -> 0; matrix products, arithmetic and copies ran while one was open for 7% -> 0% of each run, Pallas kernels for 0% -> 0%
where the time goes in v1:
time: 163 us; the launch traced here: 162 us
  Pallas kernels  153 us (94%)
  other arithmetic  5.81 us (4%)
  local copies, waits for them, and re-layouts  1.91 us (1%)
    pallas_call x1, Pallas kernels, local(): pl.pallas_call(kernel, out_shape=(jax.ShapeDtypeStruct((TOK, D), bf), jax...  153 us

profile of v1, /device:TPU:1, one launch (start us, length us, event | category | flops | bytes accessed | tf_op | source)
XLA Modules:
  0.0 161.9 jit_solution(16553265969894446013)
XLA Ops:
  0.7 0.7 convert_bitcast_fusion
  1.3 0.8 copy.9
  2.1 0.1 eq.19
  2.2 0.1 fusion
  2.3 0.2 reduce_window_sum.11
  2.5 0.2 select_reduce_fusion
  2.7 0.1 reduce_sum.12
  2.8 0.1 copy.10
  2.9 0.7 convert_bitcast_fusion.1
  3.6 1.4 maximum_select_fusion.meta
  5.0 153.5 %moe.1 = (bf16[64,7168]{1,0:T(8,128)(2,1)}, f32[128,1024]{1,0:T(8,128)}) custom-call(bf16[64,7168]{1,0:T(8,128)(2,1)} %tok.1, f32[8,128]{1,0:T(8,128)} %maximum_select_fusion.meta, bf16[896,2,1024]{2,1,0:T(2,128)(2,1)} %bitcast.7, bf16[1024,896]{1,0:T(8,128)(2,1)} %bitcast.8), custom_call_target="tpu_custom_call" | custom-call | tf_op jit(solution)/shard_map/moe/pallas_call | solution.py:412
  158.5 0.0 copy-start
  158.5 2.6 %convert_element_type.12 = f32[64,7168]{1,0:T(8,128)} convert(bf16[64,7168]{1,0:T(8,128)(2,1)} %get-tuple-element.4) | non-fusion elementwise | flops 458752 | bytes 2752512 | tf_op jit(solution)/shard_map/convert_element_type | solution.py:466
  161.1 0.0 copy-done
  161.1 0.8 copy.12
  (1 shorter events, 0.0 us)
Async XLA Ops:
  158.5 2.6 %copy-start = (f32[128,1024]{1,0:T(8,128)S(1)}, f32[128,1024]{1,0:T(8,128)}, u32[]{:S(2)}) copy-start(f32[128,1024]{1,0:T(8,128)} %get-tuple-element.5) | copy-start | bytes 1572868

commit v2 on v1

v2 whole, which is shorter than its diff:
```python
import functools

import jax
import jax.numpy as jnp
from jax import lax
from jax.experimental import pallas as pl
from jax.experimental.pallas import tpu as pltpu
from jax.sharding import PartitionSpec as P

MESH = pl.DeviceIdType.MESH
Z = 8
E = 32
TOK = 64
SLOT = 4
D = 7168
DS = D // Z
FF = 1024
ROWS = 512
HALF = 16
BLK = 32
CH = ROWS // Z
NSUB = 2
SUB = CH // NSUB
MSG = 2 * FF + 128
LEVELS = 32000.0
FAR = ((4, 3), (3, 4))
PARTS = ((0, 512), (512, 384))


def kernel(
    tok, ids, wts, w3, dn, comb_out, hess_out,
    META, T, M, DM, CT, G, X, W3V, W, DN, PRE, RSS, RSR, HD, OUT, B, CB,
    go, loc, p1s, p1r, m1s, m1r, p3s, p3r, rss, rsr, ags, agr, p8s, p8r, p10s, p10r,
):
    r = lax.axis_index("rep")
    i = lax.axis_index("exp")
    core = lax.rem(i, 2)
    pair = i // 2
    zh_own, cl_own = r // 4, lax.rem(r, 4)

    def zdev(k):
        return lax.rem(r + k + Z, Z)

    w_copy = pltpu.make_async_copy(w3, W3V, loc.at[0])
    dn_copy = pltpu.make_async_copy(dn, DN, loc.at[1])
    own_copy = pltpu.make_async_copy(
        tok.at[:, pl.ds(pl.multiple_of(r * DS, 128), DS)],
        T.at[zh_own, pl.ds(pl.multiple_of(cl_own * TOK, TOK), TOK)],
        loc.at[2],
    )
    own_copy.start()
    w_copy.start()
    dn_copy.start()

    barrier = pltpu.get_barrier_semaphore()

    @pl.loop(1, Z)
    def _(k):
        pl.semaphore_signal(barrier, inc=1, device_id=(zdev(k), i), device_id_type=MESH)

    @pl.loop(1, E)
    def _(k):
        pl.semaphore_signal(barrier, inc=1, device_id=(r, lax.rem(i + k, E)), device_id_type=MESH)

    pl.semaphore_wait(barrier, Z - 1 + E - 1)

    def tok_copy(k, part):
        to = zdev(k)
        lo, n = PARTS[part]
        return pltpu.make_async_remote_copy(
            src_ref=tok.at[:, pl.ds(pl.multiple_of(to * DS + lo, 128), n)],
            dst_ref=T.at[zh_own, pl.ds(pl.multiple_of(cl_own * TOK, TOK), TOK), pl.ds(lo, n)],
            send_sem=p1s.at[k, part],
            recv_sem=p1r.at[r, part],
            device_id=(to, i),
            device_id_type=MESH,
        )

    def meta_copy(k):
        return pltpu.make_async_remote_copy(
            src_ref=META,
            dst_ref=M.at[zh_own, cl_own],
            send_sem=m1s.at[k],
            recv_sem=m1r.at[r],
            device_id=(zdev(k), i),
            device_id_type=MESH,
        )

    def p1_send():
        for part in range(2):
            @pl.loop(1, Z)
            def _(k):
                tok_copy(k, part).start()

    def meta_send():
        row = ids[...].astype(jnp.float32)
        row = jnp.concatenate([row[0:1, :], row[1:2, :]], axis=1)
        hot = lax.broadcasted_iota(jnp.int32, (E, 2 * TOK), 0).astype(jnp.float32) == row
        hot = jnp.where(hot, 1.0, 0.0)
        earlier = lax.broadcasted_iota(jnp.int32, (2 * TOK, 2 * TOK), 0) < lax.broadcasted_iota(
            jnp.int32, (2 * TOK, 2 * TOK), 1
        )
        count = jnp.dot(
            hot.astype(jnp.bfloat16),
            jnp.where(earlier, 1.0, 0.0).astype(jnp.bfloat16),
            preferred_element_type=jnp.float32,
        )
        rank = jnp.sum(hot * count, axis=0, keepdims=True)
        pos = row * HALF + rank + (cl_own * SLOT).astype(jnp.float32)
        w = wts[...].astype(jnp.float32)
        four = jnp.concatenate([pos[:, :TOK], pos[:, TOK:], w], axis=0)
        fill = jnp.where(lax.broadcasted_iota(jnp.int32, (4, TOK), 0) < 2, -1.0, 0.0)
        wide = jnp.where(
            lax.rem(cl_own, 2) == 0,
            jnp.concatenate([four, fill], axis=1),
            jnp.concatenate([fill, four], axis=1),
        )
        META[...] = jnp.concatenate([wide, wide], axis=0)
        M[zh_own, cl_own] = jnp.concatenate([wide, wide], axis=0)

        @pl.loop(1, Z)
        def _(k):
            meta_copy(k).start()

    def meta_wait():
        @pl.loop(1, Z)
        def _(k):
            c = zdev(k)
            pltpu.make_async_remote_copy(
                src_ref=META,
                dst_ref=M.at[c // 4, lax.rem(c, 4)],
                send_sem=m1s.at[k],
                recv_sem=m1r.at[c],
                device_id=(c, i),
                device_id_type=MESH,
            ).wait_recv()

    def p1_wait(part):
        lo, n = PARTS[part]

        @pl.loop(1, Z)
        def _(k):
            c = zdev(k)
            at = pl.ds(pl.multiple_of(lax.rem(c, 4) * TOK, TOK), TOK)
            pltpu.make_async_remote_copy(
                src_ref=T.at[c // 4, at, pl.ds(lo, n)],
                dst_ref=T.at[c // 4, at, pl.ds(lo, n)],
                send_sem=p1s.at[k, part],
                recv_sem=p1r.at[c, part],
                device_id=(c, i),
                device_id_type=MESH,
            ).wait_recv()

    def routes():
        rows = lax.broadcasted_iota(jnp.int32, (ROWS, 128), 0).astype(jnp.float32)
        for zh in range(2):
            for p in range(2):
                m = jnp.maximum(M[zh, 2 * p], M[zh, 2 * p + 1])
                hit0 = rows == m[0:1, :]
                hit1 = rows == m[1:2, :]
                DM[zh, :, p * 128:(p + 1) * 128] = jnp.where(hit0 | hit1, 1.0, 0.0).astype(jnp.bfloat16)
                CT[zh, :, p * 128:(p + 1) * 128] = (
                    jnp.where(hit0, m[2:3, :], 0.0) + jnp.where(hit1, m[3:4, :], 0.0)
                ).astype(jnp.bfloat16)

    def gather(part):
        lo, n = PARTS[part]
        for zh in range(2):
            @pl.loop(0, 4)
            def _(q):
                at = pl.ds(pl.multiple_of(q * 128, 128), 128)
                got = jnp.dot(DM[zh, at, :], T[zh, :, lo:lo + n], preferred_element_type=jnp.float32)
                G[pl.ds(q * 8, 8), zh * HALF:(zh + 1) * HALF, lo:lo + n] = got.astype(jnp.bfloat16).reshape(8, HALF, n)

    def p3_copy(part, k):
        to = lax.rem(i + k, E)
        lo, n = PARTS[part]
        return pltpu.make_async_remote_copy(
            src_ref=G.at[to, :, pl.ds(lo, n)],
            dst_ref=X.at[core, pl.ds(pl.multiple_of(pair * BLK, BLK), BLK), pl.ds(lo, n)],
            send_sem=p3s.at[part],
            recv_sem=p3r.at[core, part],
            device_id=(r, to),
            device_id_type=MESH,
        )

    def p3_send(part):
        @pl.loop(1, E)
        def _(k):
            p3_copy(part, k).start()

        lo, n = PARTS[part]
        X[core, pl.ds(pl.multiple_of(pair * BLK, BLK), BLK), lo:lo + n] = G[i, :, lo:lo + n]

    def p3_sent(part):
        lo, n = PARTS[part]
        return pltpu.make_async_remote_copy(
            src_ref=G.at[pl.ds(0, E - 1), :, pl.ds(lo, n)],
            dst_ref=G.at[pl.ds(0, E - 1), :, pl.ds(lo, n)],
            send_sem=p3s.at[part],
            recv_sem=p3r.at[0, part],
            device_id=(r, lax.rem(i + 1, E)),
            device_id_type=MESH,
        )

    def p3_rows(h, part, rows):
        lo, n = PARTS[part]
        return pltpu.make_async_remote_copy(
            src_ref=X.at[h, pl.ds(0, rows), pl.ds(lo, n)],
            dst_ref=X.at[h, pl.ds(0, rows), pl.ds(lo, n)],
            send_sem=p3s.at[part],
            recv_sem=p3r.at[h, part],
            device_id=(r, lax.rem(i + 1, E)),
            device_id_type=MESH,
        )

    def p3_wait(h):
        for part in range(2):
            @pl.when(core == h)
            def _():
                p3_rows(h, part, ROWS - BLK).wait_recv()

            @pl.when(core != h)
            def _():
                p3_rows(h, part, ROWS).wait_recv()

    def p8_copy(h, p):
        return pltpu.make_async_remote_copy(
            src_ref=OUT.at[h, pl.ds(pl.multiple_of(p * BLK, BLK), BLK)],
            dst_ref=B.at[i],
            send_sem=p8s.at[h],
            recv_sem=p8r,
            device_id=(r, 2 * p + h),
            device_id_type=MESH,
        )

    def p8_wait():
        pltpu.make_async_remote_copy(
            src_ref=B.at[pl.ds(0, E - 1)],
            dst_ref=B.at[pl.ds(0, E - 1)],
            send_sem=p8s.at[0],
            recv_sem=p8r,
            device_id=(r, lax.rem(i + 1, E)),
            device_id_type=MESH,
        ).wait_recv()

    def p8_sent(h, rows):
        return pltpu.make_async_remote_copy(
            src_ref=OUT.at[h, pl.ds(0, rows)],
            dst_ref=OUT.at[h, pl.ds(0, rows)],
            send_sem=p8s.at[h],
            recv_sem=p8r,
            device_id=(r, lax.rem(i + 1, E)),
            device_id_type=MESH,
        )

    def group(owner):
        return lax.rem(owner + i, Z)

    def chunk(owner):
        return pl.ds(pl.multiple_of(group(owner) * CH, CH), CH)

    def piece(owner, sub):
        return pl.ds(pl.multiple_of(group(owner) * CH + sub * SUB, SUB), SUB)

    def up(h, owner):
        at = chunk(owner)

        @pl.loop(0, 4)
        def _(n):
            cols = pl.ds(pl.multiple_of(n * 512, 512), 512)
            PRE[h, at, cols] = jnp.dot(X[h, at, :], W[:, cols], preferred_element_type=jnp.float32)

    def up_part(h, q):
        @pl.loop(2 * q, 2 * q + 2)
        def _(n):
            cols = pl.ds(pl.multiple_of(n * 256, 256), 256)
            PRE[h, :, cols] = jnp.dot(X[h], W[:, cols], preferred_element_type=jnp.float32)

    def down(h, owner):
        at = chunk(owner)
        OUT[h, at, :] = jnp.dot(HD[h, at, :], DN[...], preferred_element_type=jnp.float32).astype(jnp.bfloat16)
        for j in range(CH // BLK):
            p = group(owner) * (CH // BLK) + j
            to = 2 * p + h

            @pl.when(to != i)
            def _():
                p8_copy(h, p).start()

            @pl.when(to == i)
            def _():
                B[i] = OUT[h, pl.ds(pl.multiple_of(pair * BLK, BLK), BLK), :]

    def rs_copy(h, way, sub, d):
        step = 1 if way == 0 else -1
        return pltpu.make_async_remote_copy(
            src_ref=RSS.at[h, way, sub, d - 1],
            dst_ref=RSR.at[h, way, sub, d - 1],
            send_sem=rss.at[h, way, sub, d - 1],
            recv_sem=rsr.at[h, way, sub, d - 1],
            device_id=(zdev(step), i),
            device_id_type=MESH,
        )

    def decode(h, way, sub, d):
        q = RSR[h, way, sub, d - 1]
        scale = jnp.exp2(q[:, 2 * FF:].astype(jnp.float32)) * (1.0 / LEVELS)
        return q, scale

    def rs_send(h, way, sub, d):
        owner = zdev(d if way == 0 else -d)
        far = FAR[h][way]
        s = PRE[h, piece(owner, sub), :]
        if d < far:
            rs_copy(h, way, sub, d + 1).wait_recv()
            q, scale = decode(h, way, sub, d + 1)
            s = s + q[:, :2 * FF].astype(jnp.float32) * jnp.tile(scale, (1, 16))
        most = jnp.maximum(jnp.max(jnp.abs(s), axis=1, keepdims=True), 1e-30)
        expo = jnp.ceil(jnp.log2(most))
        code = jnp.round(s * (jnp.exp2(-expo) * LEVELS))
        RSS[h, way, sub, d - 1, :, :2 * FF] = code.astype(jnp.int32).astype(jnp.int16)
        RSS[h, way, sub, d - 1, :, 2 * FF:] = jnp.broadcast_to(expo, (SUB, 128)).astype(jnp.int32).astype(jnp.int16)
        rs_copy(h, way, sub, d).start()

    def ag_copy(h, way, sub, k):
        step = 1 if way == 0 else -1
        origin = zdev(-(k - 1) * step)
        at = piece(origin, sub)
        return pltpu.make_async_remote_copy(
            src_ref=HD.at[h, at],
            dst_ref=HD.at[h, at],
            send_sem=ags.at[h, way, sub, k - 1],
            recv_sem=agr.at[h, way, sub, k - 1],
            device_id=(zdev(step), i),
            device_id_type=MESH,
        )

    def ag_wait(h, way, sub, k):
        step = 1 if way == 0 else -1
        origin = zdev(-k * step)
        at = piece(origin, sub)
        pltpu.make_async_remote_copy(
            src_ref=HD.at[h, at],
            dst_ref=HD.at[h, at],
            send_sem=ags.at[h, way, sub, k - 1],
            recv_sem=agr.at[h, way, sub, k - 1],
            device_id=(zdev(step), i),
            device_id_type=MESH,
        ).wait_recv()

    def finish(h, sub):
        at = piece(r, sub)
        s = PRE[h, at, :]
        for way in range(2):
            rs_copy(h, way, sub, 1).wait_recv()
            q, scale = decode(h, way, sub, 1)
            s = s + q[:, :2 * FF].astype(jnp.float32) * jnp.tile(scale, (1, 16))
        g = s[:, :FF]
        HD[h, at, :] = (g / (1.0 + jnp.exp(-g)) * s[:, FF:]).astype(jnp.bfloat16)
        for way in range(2):
            ag_copy(h, way, sub, 1).start()

    def ag_step(h, way, sub, k):
        ag_wait(h, way, sub, k)
        if k < FAR[h][way]:
            ag_copy(h, way, sub, k + 1).start()

    def combine():
        for zh in range(2):
            back = B[:, zh * HALF:(zh + 1) * HALF, :].reshape(ROWS, DS)
            CB[zh * 4 * TOK:(zh + 1) * 4 * TOK, :] = lax.dot_general(
                CT[zh], back, (((0,), (0,)), ((), ())), preferred_element_type=jnp.float32
            ).astype(jnp.bfloat16)

    mine = pl.ds(pl.multiple_of(r * DS, 128), DS)

    def p10_copy(k):
        c = zdev(k)
        return pltpu.make_async_remote_copy(
            src_ref=CB.at[pl.ds(pl.multiple_of(c * TOK, TOK), TOK)],
            dst_ref=comb_out.at[:, mine],
            send_sem=p10s.at[c],
            recv_sem=p10r.at[r],
            device_id=(c, i),
            device_id_type=MESH,
        )

    def p10_self():
        return pltpu.make_async_copy(
            CB.at[pl.ds(pl.multiple_of(r * TOK, TOK), TOK)], comb_out.at[:, mine], loc.at[3]
        )

    def p10_send(h, ks):
        @pl.when(core == h)
        def _():
            for k in ks:
                p10_copy(k).start()

    def hessian():
        at = pl.ds(pl.multiple_of(r * 128, 128), 128)
        total = lax.dot_general(
            HD[0, :, at], HD[0], (((0,), (0,)), ((), ())), preferred_element_type=jnp.float32
        ) + lax.dot_general(
            HD[1, :, at], HD[1], (((0,), (0,)), ((), ())), preferred_element_type=jnp.float32
        )
        hess_out[...] = total * (2.0 / 1024.0)

    def layout(first, last):
        @pl.loop(first, last)
        def _(n):
            at = pl.ds(pl.multiple_of(n * 64, 64), 64)
            W[at, :FF] = W3V[at, 0, :]
            W[at, FF:] = W3V[at, 1, :]

    def ag(h, k, sub):
        for way in range(2):
            if k <= FAR[h][way]:
                ag_step(h, way, sub, k)

    def downs(h, k):
        for way in range(2):
            if k <= FAR[h][way]:
                down(h, zdev(-k if way == 0 else k))

    def hand_in(part, h):
        @pl.when(core == h)
        def _():
            p1_wait(part)
            gather(part)
            p3_send(part)

    def hand_out(h):
        @pl.when(core == h)
        def _():
            p8_wait()
            combine()
            p10_self().start()

    meta_send()

    @pl.when(core == 0)
    def _():
        p1_send()

    w_copy.wait()
    layout(0, 14)
    own_copy.wait()
    meta_wait()
    routes()
    hand_in(0, 0)
    hand_in(1, 0)

    @pl.when(core == 0)
    def _():
        pl.semaphore_signal(go, inc=1, device_id=(r, i + 1), device_id_type=MESH)

    @pl.when(core == 1)
    def _():
        pl.semaphore_wait(go, 1)
        p1_send()

    p3_wait(0)
    up(0, zdev(4))
    for sub in range(NSUB):
        rs_send(0, 0, sub, 4)
    up(0, zdev(-3))
    for sub in range(NSUB):
        rs_send(0, 1, sub, 3)
    for q in range(4):
        up_part(0, q)
    hand_in(0, 1)
    for sub in range(NSUB):
        rs_send(0, 0, sub, 3)
        rs_send(0, 1, sub, 2)
    hand_in(1, 1)
    for sub in range(NSUB):
        rs_send(0, 0, sub, 2)
        rs_send(0, 1, sub, 1)
    dn_copy.wait()
    p3_wait(1)
    up(1, zdev(-4))
    for sub in range(NSUB):
        rs_send(1, 1, sub, 4)
        rs_send(0, 0, sub, 1)
    for q in range(4):
        up_part(1, q)
    for sub in range(NSUB):
        finish(0, sub)
        rs_send(1, 0, sub, 3)
        rs_send(1, 1, sub, 3)
    down(0, r)
    for sub in range(NSUB):
        ag(0, 1, sub)
        rs_send(1, 0, sub, 2)
        rs_send(1, 1, sub, 2)
    downs(0, 1)
    for sub in range(NSUB):
        ag(0, 2, sub)
        rs_send(1, 0, sub, 1)
        rs_send(1, 1, sub, 1)
    downs(0, 2)
    for sub in range(NSUB):
        ag(0, 3, sub)
        finish(1, sub)
    for sub in range(NSUB):
        ag(0, 4, sub)
    downs(0, 3)
    downs(0, 4)
    down(1, r)
    for sub in range(NSUB):
        ag(1, 1, sub)
    downs(1, 1)
    hand_out(0)
    p10_send(0, (4, 1))
    for sub in range(NSUB):
        ag(1, 2, sub)
    p10_send(0, (3, 7))
    downs(1, 2)
    for sub in range(NSUB):
        ag(1, 3, sub)
    p10_send(0, (5, 2))
    downs(1, 3)
    for sub in range(NSUB):
        ag(1, 4, sub)
    p10_send(0, (6,))
    downs(1, 4)
    hessian()
    hand_out(1)
    p10_send(1, (4, 3, 5, 2, 6, 1, 7))

    @pl.loop(1, Z)
    def _(k):
        for part in range(2):
            tok_copy(k, part).wait_send()
        meta_copy(k).wait_send()
        p10_copy(k).wait_send()

    p10_self().wait()
    for part in range(2):
        p3_sent(part).wait_send()

    for h in range(2):
        @pl.when(core == h)
        def _():
            p8_sent(h, ROWS - BLK).wait_send()

        @pl.when(core != h)
        def _():
            p8_sent(h, ROWS).wait_send()

        for way in range(2):
            for sub in range(NSUB):
                for d in range(1, FAR[h][way] + 1):
                    rs_copy(h, way, sub, d).wait_send()
                    ag_copy(h, way, sub, d).wait_send()

    @pl.loop(1, Z)
    def _(k):
        src = zdev(k)
        pltpu.make_async_remote_copy(
            src_ref=CB.at[pl.ds(0, TOK)],
            dst_ref=comb_out.at[:, pl.ds(pl.multiple_of(src * DS, 128), DS)],
            send_sem=p10s.at[src],
            recv_sem=p10r.at[src],
            device_id=(src, i),
            device_id_type=MESH,
        ).wait_recv()


def local(tokens, expert_ids, combine_weights, gate_up_weight, down_weight):
    bf, f32 = jnp.bfloat16, jnp.float32
    dma = pltpu.SemaphoreType.DMA
    comb, hess = pl.pallas_call(
        kernel,
        out_shape=(
            jax.ShapeDtypeStruct((TOK, D), bf),
            jax.ShapeDtypeStruct((128, FF), f32),
        ),
        in_specs=[
            pl.BlockSpec(memory_space=pl.ANY),
            pl.BlockSpec(memory_space=pltpu.VMEM),
            pl.BlockSpec(memory_space=pltpu.VMEM),
            pl.BlockSpec(memory_space=pl.ANY),
            pl.BlockSpec(memory_space=pl.ANY),
        ],
        out_specs=(
            pl.BlockSpec(memory_space=pl.ANY),
            pl.BlockSpec(memory_space=pltpu.VMEM),
        ),
        scratch_shapes=[
            pltpu.VMEM((8, 128), f32),
            pltpu.VMEM((2, 4 * TOK, DS), bf),
            pltpu.VMEM((2, 4, 8, 128), f32),
            pltpu.VMEM((2, ROWS, 4 * TOK), bf),
            pltpu.VMEM((2, ROWS, 4 * TOK), bf),
            pltpu.VMEM((E, BLK, DS), bf),
            pltpu.VMEM((2, ROWS, DS), bf),
            pltpu.VMEM((DS, 2, FF), bf),
            pltpu.VMEM((DS, 2 * FF), bf),
            pltpu.VMEM((FF, DS), bf),
            pltpu.VMEM((2, ROWS, 2 * FF), f32),
            pltpu.VMEM((2, 2, NSUB, 4, SUB, MSG), jnp.int16),
            pltpu.VMEM((2, 2, NSUB, 4, SUB, MSG), jnp.int16),
            pltpu.VMEM((2, ROWS, FF), bf),
            pltpu.VMEM((2, ROWS, DS), bf),
            pltpu.VMEM((E, BLK, DS), bf),
            pltpu.VMEM((Z * TOK, DS), bf),
            pltpu.SemaphoreType.REGULAR,
            dma((4,)),
            dma((Z, 2)),
            dma((Z, 2)),
            dma((Z,)),
            dma((Z,)),
            dma((2,)),
            dma((2, 2)),
            dma((2, 2, NSUB, 4)),
            dma((2, 2, NSUB, 4)),
            dma((2, 2, NSUB, 4)),
            dma((2, 2, NSUB, 4)),
            dma((2,)),
            dma,
            dma((Z,)),
            dma((Z,)),
        ],
        compiler_params=pltpu.CompilerParams(
            collective_id=0, has_side_effects=True, vmem_limit_bytes=60 * 1024 * 1024
        ),
        name="moe",
    )(tokens, expert_ids.T, combine_weights.T, gate_up_weight[0], down_weight[0])
    return comb.astype(jnp.float32), hess[None]


def solution(mesh):
    return jax.shard_map(
        local,
        mesh=mesh,
        in_specs=(
            P(("rep", "exp"), None),
            P(("rep", "exp"), None),
            P(("rep", "exp"), None),
            P("exp", "rep", None, None),
            P("exp", None, "rep"),
        ),
        out_specs=(P(("rep", "exp"), None), P("exp", "rep", None)),
        check_vma=False,
    )
```

time: 163 us -> 145 us (0.89)
  Pallas kernels: 153 us -> 141 us
  other arithmetic: 5.81 us -> 2.58 us
    pallas_call x1, Pallas kernels: 153 us -> 141 us  [local(): pl.pallas_call(kernel, out_shape=(jax.ShapeDtypeStruct((TOK, D), bf), jax...]
where the time goes in v2:
time: 145 us
  Pallas kernels  141 us (97%)
  other arithmetic  2.58 us (2%)
    pallas_call x1, Pallas kernels, local(): pl.pallas_call(kernel, out_shape=(jax.ShapeDtypeStruct((TOK, D), bf), jax...  141 us

profile of v2, /device:TPU:1, one launch (start us, length us, event | category | flops | bytes accessed | tf_op | source)
XLA Modules:
  0.0 145.1 jit_solution(6916792694867398728)
XLA Ops:
  0.6 141.1 %moe.1 = (bf16[64,7168]{1,0:T(8,128)(2,1)}, f32[128,1024]{1,0:T(8,128)}) custom-call(bf16[64,7168]{1,0:T(8,128)(2,1)} %tok.1, s32[2,64]{1,0:T(2,128)} %bitcast.8, bf16[2,64]{1,0:T(2,128)(2,1)} %bitcast.9, bf16[896,2,1024]{2,1,0:T(2,128)(2,1)} %bitcast.5, bf16[1024,896]{1,0:T(8,128)(2,1)} %bitcast.6), custom_call_target="tpu_custom_call" | custom-call | tf_op jit(solution)/shard_map/moe/pallas_call | solution.py:574
  141.7 0.0 copy-start
  141.7 2.6 %convert_element_type.3 = f32[64,7168]{1,0:T(8,128)} convert(bf16[64,7168]{1,0:T(8,128)(2,1)} %get-tuple-element.4) | non-fusion elementwise | flops 458752 | bytes 2752512 | tf_op jit(solution)/shard_map/convert_element_type | solution.py:631
  144.3 0.0 copy-done
  144.3 0.8 copy.8
Async XLA Ops:
  141.7 2.6 %copy-start = (f32[128,1024]{1,0:T(8,128)S(1)}, f32[128,1024]{1,0:T(8,128)}, u32[]{:S(2)}) copy-start(f32[128,1024]{1,0:T(8,128)} %get-tuple-element.5) | copy-start | bytes 1572868

commit v3 on v2

--- a/solution.py
+++ b/solution.py
@@ -24,7 +24,9 @@
 MSG = 2 * FF + 128
 LEVELS = 32000.0
 FAR = ((4, 3), (3, 4))
-PARTS = ((0, 512), (512, 384))
+PARTS = ((0, 256), (256, 256), (512, 256), (768, 128))
+NP = len(PARTS)
+PIECES = [(k, part) for k in (4, 3, 5, 2, 6, 1, 7) for part in range(NP)]
 
 
 def kernel(
@@ -87,7 +89,7 @@
         )
 
     def p1_send():
-        for part in range(2):
+        for part in range(NP):
             @pl.loop(1, Z)
             def _(k):
                 tok_copy(k, part).start()
@@ -215,7 +217,7 @@
         )
 
     def p3_wait(h):
-        for part in range(2):
+        for part in range(NP):
             @pl.when(core == h)
             def _():
                 p3_rows(h, part, ROWS - BLK).wait_recv()
@@ -375,27 +377,39 @@
 
     mine = pl.ds(pl.multiple_of(r * DS, 128), DS)
 
-    def p10_copy(k):
+    def p10_copy(k, part):
         c = zdev(k)
-        return pltpu.make_async_remote_copy(
-            src_ref=CB.at[pl.ds(pl.multiple_of(c * TOK, TOK), TOK)],
-            dst_ref=comb_out.at[:, mine],
+        lo, n = PARTS[part]
+        return pltpu.make_async_remote_copy(
+            src_ref=CB.at[pl.ds(pl.multiple_of(c * TOK, TOK), TOK), pl.ds(lo, n)],
+            dst_ref=comb_out.at[:, pl.ds(pl.multiple_of(r * DS + lo, 128), n)],
             send_sem=p10s.at[c],
             recv_sem=p10r.at[r],
             device_id=(c, i),
             device_id_type=MESH,
         )
 
+    def p10_all(k):
+        c = zdev(k)
+        return pltpu.make_async_remote_copy(
+            src_ref=CB.at[pl.ds(pl.multiple_of(c * TOK, TOK), TOK)],
+            dst_ref=comb_out.at[:, pl.ds(pl.multiple_of(c * DS, 128), DS)],
+            send_sem=p10s.at[c],
+            recv_sem=p10r.at[c],
+            device_id=(c, i),
+            device_id_type=MESH,
+        )
+
     def p10_self():
         return pltpu.make_async_copy(
             CB.at[pl.ds(pl.multiple_of(r * TOK, TOK), TOK)], comb_out.at[:, mine], loc.at[3]
         )
 
-    def p10_send(h, ks):
+    def p10_send(h, first, last):
         @pl.when(core == h)
         def _():
-            for k in ks:
-                p10_copy(k).start()
+            for k, part in PIECES[first:last]:
+                p10_copy(k, part).start()
 
     def hessian():
         at = pl.ds(pl.multiple_of(r * 128, 128), 128)
@@ -428,7 +442,8 @@
         def _():
             p1_wait(part)
             gather(part)
-            p3_send(part)
+            if h == 0:
+                p3_send(part)
 
     def hand_out(h):
         @pl.when(core == h)
@@ -444,12 +459,11 @@
         p1_send()
 
     w_copy.wait()
-    layout(0, 14)
+    layout(0, 8)
     own_copy.wait()
     meta_wait()
     routes()
     hand_in(0, 0)
-    hand_in(1, 0)
 
     @pl.when(core == 0)
     def _():
@@ -460,23 +474,36 @@
         pl.semaphore_wait(go, 1)
         p1_send()
 
+    for part in range(1, NP):
+        hand_in(part, 0)
+    layout(8, 14)
+    for part in range(NP - 1):
+        hand_in(part, 1)
     p3_wait(0)
+
+    @pl.when(core == 1)
+    def _():
+        for part in range(NP - 1):
+            p3_send(part)
+
     up(0, zdev(4))
     for sub in range(NSUB):
         rs_send(0, 0, sub, 4)
     up(0, zdev(-3))
     for sub in range(NSUB):
         rs_send(0, 1, sub, 3)
+    hand_in(NP - 1, 1)
+
+    @pl.when(core == 1)
+    def _():
+        p3_send(NP - 1)
+
     for q in range(4):
         up_part(0, q)
-    hand_in(0, 1)
-    for sub in range(NSUB):
-        rs_send(0, 0, sub, 3)
-        rs_send(0, 1, sub, 2)
-    hand_in(1, 1)
-    for sub in range(NSUB):
-        rs_send(0, 0, sub, 2)
-        rs_send(0, 1, sub, 1)
+    for d in (3, 2):
+        for sub in range(NSUB):
+            rs_send(0, 0, sub, d)
+            rs_send(0, 1, sub, d - 1)
     dn_copy.wait()
     p3_wait(1)
     up(1, zdev(-4))
@@ -490,54 +517,61 @@
         rs_send(1, 0, sub, 3)
         rs_send(1, 1, sub, 3)
     down(0, r)
+    ag(0, 1, 0)
+    rs_send(1, 0, 0, 2)
+    rs_send(1, 1, 0, 2)
+    ag(0, 1, 1)
+    ag(0, 2, 0)
+    downs(0, 1)
+    rs_send(1, 0, 1, 2)
+    rs_send(1, 1, 1, 2)
+    ag(0, 2, 1)
+    ag(0, 3, 0)
+    downs(0, 2)
+    rs_send(1, 0, 0, 1)
+    rs_send(1, 1, 0, 1)
+    ag(0, 3, 1)
+    ag(0, 4, 0)
+    downs(0, 3)
+    rs_send(1, 0, 1, 1)
+    rs_send(1, 1, 1, 1)
+    ag(0, 4, 1)
+    downs(0, 4)
     for sub in range(NSUB):
-        ag(0, 1, sub)
-        rs_send(1, 0, sub, 2)
-        rs_send(1, 1, sub, 2)
-    downs(0, 1)
-    for sub in range(NSUB):
-        ag(0, 2, sub)
-        rs_send(1, 0, sub, 1)
-        rs_send(1, 1, sub, 1)
-    downs(0, 2)
-    for sub in range(NSUB):
-        ag(0, 3, sub)
         finish(1, sub)
-    for sub in range(NSUB):
-        ag(0, 4, sub)
-    downs(0, 3)
-    downs(0, 4)
     down(1, r)
     for sub in range(NSUB):
         ag(1, 1, sub)
     downs(1, 1)
     hand_out(0)
-    p10_send(0, (4, 1))
-    for sub in range(NSUB):
-        ag(1, 2, sub)
-    p10_send(0, (3, 7))
+    p10_send(0, 0, 2)
+    ag(1, 2, 0)
+    p10_send(0, 2, 4)
+    ag(1, 2, 1)
+    p10_send(0, 4, 6)
     downs(1, 2)
-    for sub in range(NSUB):
-        ag(1, 3, sub)
-    p10_send(0, (5, 2))
+    ag(1, 3, 0)
+    p10_send(0, 6, 8)
+    ag(1, 3, 1)
+    p10_send(0, 8, 28)
     downs(1, 3)
     for sub in range(NSUB):
         ag(1, 4, sub)
-    p10_send(0, (6,))
     downs(1, 4)
     hessian()
     hand_out(1)
-    p10_send(1, (4, 3, 5, 2, 6, 1, 7))
+    p10_send(1, 0, 28)
 
     @pl.loop(1, Z)
     def _(k):
-        for part in range(2):
+        for part in range(NP):
             tok_copy(k, part).wait_send()
         meta_copy(k).wait_send()
-        p10_copy(k).wait_send()
+        p10_all(k).wait_send()
+        p10_all(k).wait_recv()
 
     p10_self().wait()
-    for part in range(2):
+    for part in range(NP):
         p3_sent(part).wait_send()
 
     for h in range(2):
@@ -554,18 +588,6 @@
                 for d in range(1, FAR[h][way] + 1):
                     rs_copy(h, way, sub, d).wait_send()
                     ag_copy(h, way, sub, d).wait_send()
-
-    @pl.loop(1, Z)
-    def _(k):
-        src = zdev(k)
-        pltpu.make_async_remote_copy(
-            src_ref=CB.at[pl.ds(0, TOK)],
-            dst_ref=comb_out.at[:, pl.ds(pl.multiple_of(src * DS, 128), DS)],
-            send_sem=p10s.at[src],
-            recv_sem=p10r.at[src],
-            device_id=(src, i),
-            device_id_type=MESH,
-        ).wait_recv()
 
 
 def local(tokens, expert_ids, combine_weights, gate_up_weight, down_weight):
@@ -608,12 +630,12 @@
             pltpu.VMEM((Z * TOK, DS), bf),
             pltpu.SemaphoreType.REGULAR,
             dma((4,)),
-            dma((Z, 2)),
-            dma((Z, 2)),
+            dma((Z, NP)),
+            dma((Z, NP)),
             dma((Z,)),
             dma((Z,)),
-            dma((2,)),
-            dma((2, 2)),
+            dma((NP,)),
+            dma((2, NP)),
             dma((2, 2, NSUB, 4)),
             dma((2, 2, NSUB, 4)),
             dma((2, 2, NSUB, 4)),

time: 145 us -> 135 us (0.931)
  Pallas kernels: 141 us -> 130 us
    pallas_call x1, Pallas kernels: 141 us -> 130 us  [local(): pl.pallas_call(kernel, out_shape=(jax.ShapeDtypeStruct((TOK, D), bf), jax...]
where the time goes in v3:
time: 135 us
  Pallas kernels  130 us (96%)
  other arithmetic  2.58 us (2%)
    pallas_call x1, Pallas kernels, local(): pl.pallas_call(kernel, out_shape=(jax.ShapeDtypeStruct((TOK, D), bf), jax...  130 us

profile of v3, /device:TPU:1, one launch (start us, length us, event | category | flops | bytes accessed | tf_op | source)
XLA Modules:
  0.0 134.5 jit_solution(8603614720386064679)
XLA Ops:
  0.6 130.5 %moe.1 = (bf16[64,7168]{1,0:T(8,128)(2,1)}, f32[128,1024]{1,0:T(8,128)}) custom-call(bf16[64,7168]{1,0:T(8,128)(2,1)} %tok.1, s32[2,64]{1,0:T(2,128)} %bitcast.8, bf16[2,64]{1,0:T(2,128)(2,1)} %bitcast.9, bf16[896,2,1024]{2,1,0:T(2,128)(2,1)} %bitcast.5, bf16[1024,896]{1,0:T(8,128)(2,1)} %bitcast.6), custom_call_target="tpu_custom_call" | custom-call | tf_op jit(solution)/shard_map/moe/pallas_call | solution.py:596
  131.1 0.0 copy-start
  131.1 2.6 %convert_element_type.3 = f32[64,7168]{1,0:T(8,128)} convert(bf16[64,7168]{1,0:T(8,128)(2,1)} %get-tuple-element.4) | non-fusion elementwise | flops 458752 | bytes 2752512 | tf_op jit(solution)/shard_map/convert_element_type | solution.py:653
  133.7 0.0 copy-done
  133.7 0.8 copy.8
Async XLA Ops:
  131.1 2.6 %copy-start = (f32[128,1024]{1,0:T(8,128)S(1)}, f32[128,1024]{1,0:T(8,128)}, u32[]{:S(2)}) copy-start(f32[128,1024]{1,0:T(8,128)} %get-tuple-element.5) | copy-start | bytes 1572868

commit v4 on v3

--- a/solution.py
+++ b/solution.py
@@ -24,21 +24,22 @@
 MSG = 2 * FF + 128
 LEVELS = 32000.0
 FAR = ((4, 3), (3, 4))
-PARTS = ((0, 256), (256, 256), (512, 256), (768, 128))
+PARTS = ((0, 128), (128, 256), (384, 256), (640, 256))
 NP = len(PARTS)
-PIECES = [(k, part) for k in (4, 3, 5, 2, 6, 1, 7) for part in range(NP)]
+PIECES = [(q, part) for part in range(NP) for q in range(4)]
 
 
 def kernel(
     tok, ids, wts, w3, dn, comb_out, hess_out,
-    META, T, M, DM, CT, G, X, W3V, W, DN, PRE, RSS, RSR, HD, OUT, B, CB,
-    go, loc, p1s, p1r, m1s, m1r, p3s, p3r, rss, rsr, ags, agr, p8s, p8r, p10s, p10r,
+    META, T, M, MS, DM, CT, G, X, W3V, W, DN, PRE, RSS, RSR, HD, OUT, B, CB,
+    go, sibs, sibr, loc, p1s, p1r, m1s, m1r, p3s, p3r, rss, rsr, ags, agr, p8s, p8r, p10s, p10r,
 ):
     r = lax.axis_index("rep")
     i = lax.axis_index("exp")
     core = lax.rem(i, 2)
     pair = i // 2
-    zh_own, cl_own = r // 4, lax.rem(r, 4)
+    sib = i + 1 - 2 * core
+    zh_own, cl_own = lax.rem(r, 2), r // 2
 
     def zdev(k):
         return lax.rem(r + k + Z, Z)
@@ -59,12 +60,13 @@
     @pl.loop(1, Z)
     def _(k):
         pl.semaphore_signal(barrier, inc=1, device_id=(zdev(k), i), device_id_type=MESH)
+        pl.semaphore_signal(barrier, inc=1, device_id=(zdev(k), sib), device_id_type=MESH)
 
     @pl.loop(1, E)
     def _(k):
         pl.semaphore_signal(barrier, inc=1, device_id=(r, lax.rem(i + k, E)), device_id_type=MESH)
 
-    pl.semaphore_wait(barrier, Z - 1 + E - 1)
+    pl.semaphore_wait(barrier, 2 * (Z - 1) + E - 1)
 
     def tok_copy(k, part):
         to = zdev(k)
@@ -130,7 +132,7 @@
             c = zdev(k)
             pltpu.make_async_remote_copy(
                 src_ref=META,
-                dst_ref=M.at[c // 4, lax.rem(c, 4)],
+                dst_ref=M.at[lax.rem(c, 2), c // 2],
                 send_sem=m1s.at[k],
                 recv_sem=m1r.at[c],
                 device_id=(c, i),
@@ -143,27 +145,44 @@
         @pl.loop(1, Z)
         def _(k):
             c = zdev(k)
-            at = pl.ds(pl.multiple_of(lax.rem(c, 4) * TOK, TOK), TOK)
+            at = pl.ds(pl.multiple_of((c // 2) * TOK, TOK), TOK)
+            zh = lax.rem(c, 2)
             pltpu.make_async_remote_copy(
-                src_ref=T.at[c // 4, at, pl.ds(lo, n)],
-                dst_ref=T.at[c // 4, at, pl.ds(lo, n)],
+                src_ref=T.at[zh, at, pl.ds(lo, n)],
+                dst_ref=T.at[zh, at, pl.ds(lo, n)],
                 send_sem=p1s.at[k, part],
                 recv_sem=p1r.at[c, part],
                 device_id=(c, i),
                 device_id_type=MESH,
             ).wait_recv()
 
+    sib_copy = pltpu.make_async_remote_copy(
+        src_ref=M.at[1], dst_ref=MS, send_sem=sibs, recv_sem=sibr, device_id=(r, sib), device_id_type=MESH
+    )
+
+    def hits(m):
+        rows = lax.broadcasted_iota(jnp.int32, (ROWS, 128), 0).astype(jnp.float32)
+        return rows == m[0:1, :], rows == m[1:2, :]
+
+    def weights(which, p, m):
+        hit0, hit1 = hits(m)
+        CT[which, :, p * 128:(p + 1) * 128] = (
+            jnp.where(hit0, m[2:3, :], 0.0) + jnp.where(hit1, m[3:4, :], 0.0)
+        ).astype(jnp.bfloat16)
+
     def routes():
-        rows = lax.broadcasted_iota(jnp.int32, (ROWS, 128), 0).astype(jnp.float32)
-        for zh in range(2):
-            for p in range(2):
+        sib_copy.start()
+        for p in range(2):
+            for zh in range(2):
                 m = jnp.maximum(M[zh, 2 * p], M[zh, 2 * p + 1])
-                hit0 = rows == m[0:1, :]
-                hit1 = rows == m[1:2, :]
+                hit0, hit1 = hits(m)
                 DM[zh, :, p * 128:(p + 1) * 128] = jnp.where(hit0 | hit1, 1.0, 0.0).astype(jnp.bfloat16)
-                CT[zh, :, p * 128:(p + 1) * 128] = (
-                    jnp.where(hit0, m[2:3, :], 0.0) + jnp.where(hit1, m[3:4, :], 0.0)
-                ).astype(jnp.bfloat16)
+
+    def returns():
+        sib_copy.wait_recv()
+        for p in range(2):
+            weights(0, p, jnp.maximum(M[0, 2 * p], M[0, 2 * p + 1]))
+            weights(1, p, jnp.maximum(MS[2 * p], MS[2 * p + 1]))
 
     def gather(part):
         lo, n = PARTS[part]
@@ -226,33 +245,34 @@
             def _():
                 p3_rows(h, part, ROWS).wait_recv()
 
-    def p8_copy(h, p):
-        return pltpu.make_async_remote_copy(
-            src_ref=OUT.at[h, pl.ds(pl.multiple_of(p * BLK, BLK), BLK)],
-            dst_ref=B.at[i],
+    def p8_copy(h, p, zh):
+        return pltpu.make_async_remote_copy(
+            src_ref=OUT.at[h, pl.ds(pl.multiple_of(p * BLK + zh * HALF, HALF), HALF)],
+            dst_ref=B.at[h, i],
             send_sem=p8s.at[h],
-            recv_sem=p8r,
-            device_id=(r, 2 * p + h),
-            device_id_type=MESH,
-        )
-
-    def p8_wait():
+            recv_sem=p8r.at[h],
+            device_id=(r, 2 * p + (h if zh == 0 else 1 - h)),
+            device_id_type=MESH,
+        )
+
+    def p8_wait(h):
         pltpu.make_async_remote_copy(
-            src_ref=B.at[pl.ds(0, E - 1)],
-            dst_ref=B.at[pl.ds(0, E - 1)],
-            send_sem=p8s.at[0],
-            recv_sem=p8r,
-            device_id=(r, lax.rem(i + 1, E)),
+            src_ref=B.at[h, pl.ds(0, E - 1)],
+            dst_ref=B.at[h, pl.ds(0, E - 1)],
+            send_sem=p8s.at[h],
+            recv_sem=p8r.at[h],
+            device_id=(r, sib),
             device_id_type=MESH,
         ).wait_recv()
 
-    def p8_sent(h, rows):
-        return pltpu.make_async_remote_copy(
-            src_ref=OUT.at[h, pl.ds(0, rows)],
-            dst_ref=OUT.at[h, pl.ds(0, rows)],
+    def p8_sent(h):
+        most = pl.ds(0, (E - 1) * HALF)
+        return pltpu.make_async_remote_copy(
+            src_ref=OUT.at[h, most],
+            dst_ref=OUT.at[h, most],
             send_sem=p8s.at[h],
-            recv_sem=p8r,
-            device_id=(r, lax.rem(i + 1, E)),
+            recv_sem=p8r.at[h],
+            device_id=(r, sib),
             device_id_type=MESH,
         )
 
@@ -272,6 +292,17 @@
         def _(n):
             cols = pl.ds(pl.multiple_of(n * 512, 512), 512)
             PRE[h, at, cols] = jnp.dot(X[h, at, :], W[:, cols], preferred_element_type=jnp.float32)
+
+    def up_two(h, first, second):
+        one, two = chunk(first), chunk(second)
+
+        @pl.loop(0, 4)
+        def _(n):
+            cols = pl.ds(pl.multiple_of(n * 512, 512), 512)
+            rows = jnp.concatenate([X[h, one, :], X[h, two, :]], axis=0)
+            got = jnp.dot(rows, W[:, cols], preferred_element_type=jnp.float32)
+            PRE[h, one, cols] = got[:CH]
+            PRE[h, two, cols] = got[CH:]
 
     def up_part(h, q):
         @pl.loop(2 * q, 2 * q + 2)
@@ -284,15 +315,16 @@
         OUT[h, at, :] = jnp.dot(HD[h, at, :], DN[...], preferred_element_type=jnp.float32).astype(jnp.bfloat16)
         for j in range(CH // BLK):
             p = group(owner) * (CH // BLK) + j
-            to = 2 * p + h
-
-            @pl.when(to != i)
-            def _():
-                p8_copy(h, p).start()
-
-            @pl.when(to == i)
-            def _():
-                B[i] = OUT[h, pl.ds(pl.multiple_of(pair * BLK, BLK), BLK), :]
+            for zh in range(2):
+                to = 2 * p + (h if zh == 0 else 1 - h)
+
+                @pl.when(to != i)
+                def _():
+                    p8_copy(h, p, zh).start()
+
+                @pl.when(to == i)
+                def _():
+                    B[h, i] = OUT[h, pl.ds(pl.multiple_of(pair * BLK + zh * HALF, HALF), HALF), :]
 
     def rs_copy(h, way, sub, d):
         step = 1 if way == 0 else -1
@@ -368,48 +400,44 @@
         if k < FAR[h][way]:
             ag_copy(h, way, sub, k + 1).start()
 
-    def combine():
-        for zh in range(2):
-            back = B[:, zh * HALF:(zh + 1) * HALF, :].reshape(ROWS, DS)
-            CB[zh * 4 * TOK:(zh + 1) * 4 * TOK, :] = lax.dot_general(
-                CT[zh], back, (((0,), (0,)), ((), ())), preferred_element_type=jnp.float32
-            ).astype(jnp.bfloat16)
+    def whose(h):
+        return lax.rem(core + h, 2)
+
+    def combine(h):
+        CB[h] = lax.dot_general(
+            CT[whose(h)], B[h].reshape(ROWS, DS), (((0,), (0,)), ((), ())), preferred_element_type=jnp.float32
+        ).astype(jnp.bfloat16)
 
     mine = pl.ds(pl.multiple_of(r * DS, 128), DS)
 
-    def p10_copy(k, part):
-        c = zdev(k)
+    def p10_copy(h, q, part):
+        w = whose(h)
+        cl = lax.rem(q + r // 2, 4)
         lo, n = PARTS[part]
         return pltpu.make_async_remote_copy(
-            src_ref=CB.at[pl.ds(pl.multiple_of(c * TOK, TOK), TOK), pl.ds(lo, n)],
+            src_ref=CB.at[h, pl.ds(pl.multiple_of(cl * TOK, TOK), TOK), pl.ds(lo, n)],
             dst_ref=comb_out.at[:, pl.ds(pl.multiple_of(r * DS + lo, 128), n)],
-            send_sem=p10s.at[c],
+            send_sem=p10s.at[h, cl],
             recv_sem=p10r.at[r],
-            device_id=(c, i),
-            device_id_type=MESH,
-        )
-
-    def p10_all(k):
-        c = zdev(k)
-        return pltpu.make_async_remote_copy(
-            src_ref=CB.at[pl.ds(pl.multiple_of(c * TOK, TOK), TOK)],
-            dst_ref=comb_out.at[:, pl.ds(pl.multiple_of(c * DS, 128), DS)],
-            send_sem=p10s.at[c],
-            recv_sem=p10r.at[c],
-            device_id=(c, i),
-            device_id_type=MESH,
-        )
+            device_id=(2 * cl + w, i + w * (sib - i)),
+            device_id_type=MESH,
+        )
+
+    def p10_away(h, q):
+        w = whose(h)
+        cl = lax.rem(q + r // 2, 4)
+        return jnp.logical_or(w == 1, 2 * cl + w != r)
 
     def p10_self():
         return pltpu.make_async_copy(
-            CB.at[pl.ds(pl.multiple_of(r * TOK, TOK), TOK)], comb_out.at[:, mine], loc.at[3]
+            CB.at[core, pl.ds(pl.multiple_of((r // 2) * TOK, TOK), TOK)], comb_out.at[:, mine], loc.at[3]
         )
 
     def p10_send(h, first, last):
-        @pl.when(core == h)
-        def _():
-            for k, part in PIECES[first:last]:
-                p10_copy(k, part).start()
+        for q, part in PIECES[first:last]:
+            @pl.when(p10_away(h, q))
+            def _():
+                p10_copy(h, q, part).start()
 
     def hessian():
         at = pl.ds(pl.multiple_of(r * 128, 128), 128)
@@ -446,10 +474,11 @@
                 p3_send(part)
 
     def hand_out(h):
-        @pl.when(core == h)
+        p8_wait(h)
+        combine(h)
+
+        @pl.when(jnp.logical_and(core == h, lax.rem(r, 2) == 0))
         def _():
-            p8_wait()
-            combine()
             p10_self().start()
 
     meta_send()
@@ -464,6 +493,7 @@
     meta_wait()
     routes()
     hand_in(0, 0)
+    hand_in(1, 0)
 
     @pl.when(core == 0)
     def _():
@@ -474,8 +504,9 @@
         pl.semaphore_wait(go, 1)
         p1_send()
 
-    for part in range(1, NP):
+    for part in range(2, NP):
         hand_in(part, 0)
+    returns()
     layout(8, 14)
     for part in range(NP - 1):
         hand_in(part, 1)
@@ -486,11 +517,9 @@
         for part in range(NP - 1):
             p3_send(part)
 
-    up(0, zdev(4))
+    up_two(0, zdev(4), zdev(-3))
     for sub in range(NSUB):
         rs_send(0, 0, sub, 4)
-    up(0, zdev(-3))
-    for sub in range(NSUB):
         rs_send(0, 1, sub, 3)
     hand_in(NP - 1, 1)
 
@@ -543,51 +572,71 @@
     for sub in range(NSUB):
         ag(1, 1, sub)
     downs(1, 1)
-    hand_out(0)
-    p10_send(0, 0, 2)
     ag(1, 2, 0)
-    p10_send(0, 2, 4)
     ag(1, 2, 1)
-    p10_send(0, 4, 6)
     downs(1, 2)
     ag(1, 3, 0)
-    p10_send(0, 6, 8)
     ag(1, 3, 1)
-    p10_send(0, 8, 28)
+    hand_out(0)
+    p10_send(0, 0, 6)
     downs(1, 3)
     for sub in range(NSUB):
         ag(1, 4, sub)
     downs(1, 4)
+    p10_send(0, 6, 16)
     hessian()
     hand_out(1)
-    p10_send(1, 0, 28)
+    p10_send(1, 0, 16)
 
     @pl.loop(1, Z)
     def _(k):
         for part in range(NP):
             tok_copy(k, part).wait_send()
         meta_copy(k).wait_send()
-        p10_all(k).wait_send()
-        p10_all(k).wait_recv()
-
-    p10_self().wait()
+
+    sib_copy.wait_send()
     for part in range(NP):
         p3_sent(part).wait_send()
 
     for h in range(2):
-        @pl.when(core == h)
-        def _():
-            p8_sent(h, ROWS - BLK).wait_send()
-
-        @pl.when(core != h)
-        def _():
-            p8_sent(h, ROWS).wait_send()
-
+        p8_sent(h).wait_send()
         for way in range(2):
             for sub in range(NSUB):
                 for d in range(1, FAR[h][way] + 1):
                     rs_copy(h, way, sub, d).wait_send()
                     ag_copy(h, way, sub, d).wait_send()
+        for q in range(4):
+            cl = lax.rem(q + r // 2, 4)
+
+            @pl.when(p10_away(h, q))
+            def _():
+                pltpu.make_async_remote_copy(
+                    src_ref=CB.at[h, pl.ds(pl.multiple_of(cl * TOK, TOK), TOK)],
+                    dst_ref=comb_out.at[:, mine],
+                    send_sem=p10s.at[h, cl],
+                    recv_sem=p10r.at[r],
+                    device_id=(r, sib),
+                    device_id_type=MESH,
+                ).wait_send()
+
+    @pl.when(lax.rem(r, 2) == 0)
+    def _():
+        p10_self().wait()
+
+    @pl.loop(0, Z)
+    def _(k):
+        c = zdev(k)
+
+        @pl.when(jnp.logical_or(lax.rem(r, 2) == 1, k != 0))
+        def _():
+            pltpu.make_async_remote_copy(
+                src_ref=CB.at[0, pl.ds(0, TOK)],
+                dst_ref=comb_out.at[:, pl.ds(pl.multiple_of(c * DS, 128), DS)],
+                send_sem=p10s.at[0, 0],
+                recv_sem=p10r.at[c],
+                device_id=(r, sib),
+                device_id_type=MESH,
+            ).wait_recv()
 
 
 def local(tokens, expert_ids, combine_weights, gate_up_weight, down_weight):
@@ -614,6 +663,7 @@
             pltpu.VMEM((8, 128), f32),
             pltpu.VMEM((2, 4 * TOK, DS), bf),
             pltpu.VMEM((2, 4, 8, 128), f32),
+            pltpu.VMEM((4, 8, 128), f32),
             pltpu.VMEM((2, ROWS, 4 * TOK), bf),
             pltpu.VMEM((2, ROWS, 4 * TOK), bf),
             pltpu.VMEM((E, BLK, DS), bf),
@@ -626,9 +676,11 @@
             pltpu.VMEM((2, 2, NSUB, 4, SUB, MSG), jnp.int16),
             pltpu.VMEM((2, ROWS, FF), bf),
             pltpu.VMEM((2, ROWS, DS), bf),
-            pltpu.VMEM((E, BLK, DS), bf),
-            pltpu.VMEM((Z * TOK, DS), bf),
+            pltpu.VMEM((2, E, HALF, DS), bf),
+            pltpu.VMEM((2, 4 * TOK, DS), bf),
             pltpu.SemaphoreType.REGULAR,
+            dma,
+            dma,
             dma((4,)),
             dma((Z, NP)),
             dma((Z, NP)),
@@ -641,8 +693,8 @@
             dma((2, 2, NSUB, 4)),
             dma((2, 2, NSUB, 4)),
             dma((2,)),
-            dma,
-            dma((Z,)),
+            dma((2,)),
+            dma((2, 4)),
             dma((Z,)),
         ],
         compiler_params=pltpu.CompilerParams(

time: 135 us -> 133 us (0.985)
  no operation moved by 1% of the time
where the time goes in v4:
time: 133 us
  Pallas kernels  129 us (97%)
  other arithmetic  2.58 us (2%)
    pallas_call x1, Pallas kernels, local(): pl.pallas_call(kernel, out_shape=(jax.ShapeDtypeStruct((TOK, D), bf), jax...  129 us

profile of v4, /device:TPU:1, one launch (start us, length us, event | category | flops | bytes accessed | tf_op | source)
XLA Modules:
  0.0 133.2 jit_solution(2726196984011423534)
XLA Ops:
  0.6 129.2 %moe.1 = (bf16[64,7168]{1,0:T(8,128)(2,1)}, f32[128,1024]{1,0:T(8,128)}) custom-call(bf16[64,7168]{1,0:T(8,128)(2,1)} %tok.1, s32[2,64]{1,0:T(2,128)} %bitcast.8, bf16[2,64]{1,0:T(2,128)(2,1)} %bitcast.9, bf16[896,2,1024]{2,1,0:T(2,128)(2,1)} %bitcast.5, bf16[1024,896]{1,0:T(8,128)(2,1)} %bitcast.6), custom_call_target="tpu_custom_call" | custom-call | tf_op jit(solution)/shard_map/moe/pallas_call | solution.py:645
  129.8 0.0 copy-start
  129.8 2.6 %convert_element_type.3 = f32[64,7168]{1,0:T(8,128)} convert(bf16[64,7168]{1,0:T(8,128)(2,1)} %get-tuple-element.4) | non-fusion elementwise | flops 458752 | bytes 2752512 | tf_op jit(solution)/shard_map/convert_element_type | solution.py:705
  132.4 0.0 copy-done
  132.4 0.8 copy.8
Async XLA Ops:
  129.8 2.6 %copy-start = (f32[128,1024]{1,0:T(8,128)S(1)}, f32[128,1024]{1,0:T(8,128)}, u32[]{:S(2)}) copy-start(f32[128,1024]{1,0:T(8,128)} %get-tuple-element.5) | copy-start | bytes 1572868

commit v5 on v4

--- a/solution.py
+++ b/solution.py
@@ -21,7 +21,8 @@
 CH = ROWS // Z
 NSUB = 2
 SUB = CH // NSUB
-MSG = 2 * FF + 128
+LANES = 2 * FF // 128
+TILES = 2 * LANES + 1
 LEVELS = 32000.0
 FAR = ((4, 3), (3, 4))
 PARTS = ((0, 128), (128, 256), (384, 256), (640, 256))
@@ -338,9 +339,17 @@
         )
 
     def decode(h, way, sub, d):
-        q = RSR[h, way, sub, d - 1]
-        scale = jnp.exp2(q[:, 2 * FF:].astype(jnp.float32)) * (1.0 / LEVELS)
-        return q, scale
+        at = (h, way, sub, d - 1)
+        expo = RSR[at + (TILES - 1,)].astype(jnp.float32)
+        expo = jnp.concatenate([expo[:, 0:1], expo[:, 64:65]], axis=0)
+        scale = jnp.broadcast_to(jnp.exp2(expo) * (1.0 / LEVELS), (SUB, 128))
+        return jnp.concatenate(
+            [
+                RSR[at + (slice(2 * c, 2 * c + 2),)].reshape(SUB, 128).astype(jnp.float32) * scale
+                for c in range(LANES)
+            ],
+            axis=1,
+        )
 
     def rs_send(h, way, sub, d):
         owner = zdev(d if way == 0 else -d)
@@ -348,13 +357,16 @@
         s = PRE[h, piece(owner, sub), :]
         if d < far:
             rs_copy(h, way, sub, d + 1).wait_recv()
-            q, scale = decode(h, way, sub, d + 1)
-            s = s + q[:, :2 * FF].astype(jnp.float32) * jnp.tile(scale, (1, 16))
+            s = s + decode(h, way, sub, d + 1)
         most = jnp.maximum(jnp.max(jnp.abs(s), axis=1, keepdims=True), 1e-30)
         expo = jnp.ceil(jnp.log2(most))
         code = jnp.round(s * (jnp.exp2(-expo) * LEVELS))
-        RSS[h, way, sub, d - 1, :, :2 * FF] = code.astype(jnp.int32).astype(jnp.int16)
-        RSS[h, way, sub, d - 1, :, 2 * FF:] = jnp.broadcast_to(expo, (SUB, 128)).astype(jnp.int32).astype(jnp.int16)
+        code = code.astype(jnp.int32).astype(jnp.int16)
+        for c in range(LANES):
+            RSS[h, way, sub, d - 1, 2 * c:2 * c + 2] = code[:, c * 128:(c + 1) * 128].reshape(2, 16, 128)
+        wide = jnp.broadcast_to(expo, (SUB, 128))
+        low = lax.broadcasted_iota(jnp.int32, (16, 128), 1) < 64
+        RSS[h, way, sub, d - 1, TILES - 1] = jnp.where(low, wide[:16], wide[16:]).astype(jnp.int32).astype(jnp.int16)
         rs_copy(h, way, sub, d).start()
 
     def ag_copy(h, way, sub, k):
@@ -388,8 +400,7 @@
         s = PRE[h, at, :]
         for way in range(2):
             rs_copy(h, way, sub, 1).wait_recv()
-            q, scale = decode(h, way, sub, 1)
-            s = s + q[:, :2 * FF].astype(jnp.float32) * jnp.tile(scale, (1, 16))
+            s = s + decode(h, way, sub, 1)
         g = s[:, :FF]
         HD[h, at, :] = (g / (1.0 + jnp.exp(-g)) * s[:, FF:]).astype(jnp.bfloat16)
         for way in range(2):
@@ -672,8 +683,8 @@
             pltpu.VMEM((DS, 2 * FF), bf),
             pltpu.VMEM((FF, DS), bf),
             pltpu.VMEM((2, ROWS, 2 * FF), f32),
-            pltpu.VMEM((2, 2, NSUB, 4, SUB, MSG), jnp.int16),
-            pltpu.VMEM((2, 2, NSUB, 4, SUB, MSG), jnp.int16),
+            pltpu.VMEM((2, 2, NSUB, 4, TILES, 16, 128), jnp.int16),
+            pltpu.VMEM((2, 2, NSUB, 4, TILES, 16, 128), jnp.int16),
             pltpu.VMEM((2, ROWS, FF), bf),
             pltpu.VMEM((2, ROWS, DS), bf),
             pltpu.VMEM((2, E, HALF, DS), bf),

time: 133 us -> 133 us (level)
  no operation moved by 1% of the time
where the time goes in v5:
time: 133 us
  Pallas kernels  129 us (97%)
  other arithmetic  2.58 us (2%)
    pallas_call x1, Pallas kernels, local(): pl.pallas_call(kernel, out_shape=(jax.ShapeDtypeStruct((TOK, D), bf), jax...  129 us

profile of v5, /device:TPU:1, one launch (start us, length us, event | category | flops | bytes accessed | tf_op | source)
XLA Modules:
  0.0 132.7 jit_solution(4439693633500355071)
XLA Ops:
  0.6 128.6 %moe.1 = (bf16[64,7168]{1,0:T(8,128)(2,1)}, f32[128,1024]{1,0:T(8,128)}) custom-call(bf16[64,7168]{1,0:T(8,128)(2,1)} %tok.1, s32[2,64]{1,0:T(2,128)} %bitcast.8, bf16[2,64]{1,0:T(2,128)(2,1)} %bitcast.9, bf16[896,2,1024]{2,1,0:T(2,128)(2,1)} %bitcast.5, bf16[1024,896]{1,0:T(8,128)(2,1)} %bitcast.6), custom_call_target="tpu_custom_call" | custom-call | tf_op jit(solution)/shard_map/moe/pallas_call | solution.py:656
  129.3 0.0 copy-start
  129.3 2.6 %convert_element_type.3 = f32[64,7168]{1,0:T(8,128)} convert(bf16[64,7168]{1,0:T(8,128)(2,1)} %get-tuple-element.4) | non-fusion elementwise | flops 458752 | bytes 2752512 | tf_op jit(solution)/shard_map/convert_element_type | solution.py:716
  131.9 0.0 copy-done
  131.9 0.8 copy.8
Async XLA Ops:
  129.3 2.6 %copy-start = (f32[128,1024]{1,0:T(8,128)S(1)}, f32[128,1024]{1,0:T(8,128)}, u32[]{:S(2)}) copy-start(f32[128,1024]{1,0:T(8,128)} %get-tuple-element.5) | copy-start | bytes 1572868

commit v6 on v5

--- a/solution.py
+++ b/solution.py
@@ -504,7 +504,6 @@
     meta_wait()
     routes()
     hand_in(0, 0)
-    hand_in(1, 0)
 
     @pl.when(core == 0)
     def _():
@@ -515,7 +514,7 @@
         pl.semaphore_wait(go, 1)
         p1_send()
 
-    for part in range(2, NP):
+    for part in range(1, NP):
         hand_in(part, 0)
     returns()
     layout(8, 14)

time: 133 us -> 135 us (1.015)
    pallas_call x1, Pallas kernels: 129 us -> 130 us  [local(): pl.pallas_call(kernel, out_shape=(jax.ShapeDtypeStruct((TOK, D), bf), jax...]
where the time goes in v6:
time: 135 us
  Pallas kernels  130 us (96%)
  other arithmetic  2.58 us (2%)
    pallas_call x1, Pallas kernels, local(): pl.pallas_call(kernel, out_shape=(jax.ShapeDtypeStruct((TOK, D), bf), jax...  130 us

profile of v6, /device:TPU:1, one launch (start us, length us, event | category | flops | bytes accessed | tf_op | source)
XLA Modules:
  0.0 134.5 jit_solution(13735359990300604527)
XLA Ops:
  0.6 130.5 %moe.1 = (bf16[64,7168]{1,0:T(8,128)(2,1)}, f32[128,1024]{1,0:T(8,128)}) custom-call(bf16[64,7168]{1,0:T(8,128)(2,1)} %tok.1, s32[2,64]{1,0:T(2,128)} %bitcast.8, bf16[2,64]{1,0:T(2,128)(2,1)} %bitcast.9, bf16[896,2,1024]{2,1,0:T(2,128)(2,1)} %bitcast.5, bf16[1024,896]{1,0:T(8,128)(2,1)} %bitcast.6), custom_call_target="tpu_custom_call" | custom-call | tf_op jit(solution)/shard_map/moe/pallas_call | solution.py:655
  131.1 0.0 copy-start
  131.1 2.6 %convert_element_type.3 = f32[64,7168]{1,0:T(8,128)} convert(bf16[64,7168]{1,0:T(8,128)(2,1)} %get-tuple-element.4) | non-fusion elementwise | flops 458752 | bytes 2752512 | tf_op jit(solution)/shard_map/convert_element_type | solution.py:715
  133.7 0.0 copy-done
  133.7 0.8 copy.8
Async XLA Ops:
  131.1 2.6 %copy-start = (f32[128,1024]{1,0:T(8,128)S(1)}, f32[128,1024]{1,0:T(8,128)}, u32[]{:S(2)}) copy-start(f32[128,1024]{1,0:T(8,128)} %get-tuple-element.5) | copy-start | bytes 1572868
